TPU v7x, 128 devices: a whole 4x4x4 slice. The times are simulated.
128 devices in a mesh: brick: 16 (over z, y), gz: 8 (over x, core).
Axes of the slice: x: 4, y: 4, z: 4, core: 2. Of those that a mesh axis runs over, the one named last changes fastest.
Arguments:
- point_spots: float32 [8, 4096, 3, 128], P('gz', 'brick'), may hold values from 0 to 1
- point_values: float32 [8, 4096, 2, 128], P('gz', 'brick'), may hold values from -12 to 12
- dest_brick: int32 [8, 4096, 1], P('gz', 'brick'), may hold values from 0 to 15; in each aligned block of 256 rows (0 to 255, 256 to 511, ..., all dimensions but the last counted through in order) at most 24 rows name the same one
- dest_tile: int32 [8, 4096], P('gz', 'brick'), may hold values from 0 to 127
- live_count: int32 [8, 4096], P('gz', 'brick'), may hold values from 1 to 128, 393216 in all within a row
Outputs:
- density: float32 [2, 512, 512, 512], P(None, ('brick', 'gz'))
Inputs may be any that keep to these rules, and one draw needn't show every extreme that they name: `dest_brick`: among the blocks of one device, at most 24 name the same brick, a bound that some block reaches of them.
All inputs are finite; a program needn't handle non-finite values. No bound on the sum of `live_count` on one device may be relied on, other than what follows from the above.
Results may differ from a plain program's by a relative error of at most 0.0043.
Values sent between devices are 32-bit elements; how exact they have to be, the bound alone decides.
No kernel may reach another device: no remote copies, remote signals or barrier semaphores. Data moves between devices by JAX's collectives and lax.ppermute only.
A program may use at most 128 MiB of HBM per device.

v0:
```python
import math

import jax
import jax.numpy as jnp
from jax import lax
from jax.sharding import PartitionSpec as P

GRID = 512
TX = 16
TZ = 4


def kernel(spread_t):
    return jnp.maximum(0.0, 1.0 - spread_t * spread_t / 4.0) ** 10


def correction(length):
    places = jnp.arange(length, dtype=jnp.int32)
    shifted = jnp.where(places < length // 2, places, places - length)
    sample_nodes = jnp.arange(-63, 64, dtype=jnp.int32)
    phases = (shifted[:, None] * sample_nodes[None, :]).astype(jnp.float32) * (
        2.0 * math.pi / (32.0 * length)
    )
    weights = kernel(sample_nodes.astype(jnp.float32) / 32.0)
    return jnp.sum(weights[None, :] * jnp.cos(phases), axis=1) / 32.0


def tables(length):
    places = jnp.arange(length, dtype=jnp.int32)
    turned = places[:, None] * places[None, :] % length
    angles = turned.astype(jnp.float32) * (2.0 * math.pi / length)
    cosine = jnp.cos(angles)
    sine_part = jnp.sin(angles)
    return (cosine, sine_part)


def rotate(einsum_form, real_part, imag_part, cosine, sine_part):

    def contract(left_side, right_side):
        return jnp.einsum(
            einsum_form,
            left_side,
            right_side,
            precision=lax.Precision.HIGHEST,
            preferred_element_type=jnp.float32,
        )

    return jnp.stack(
        [
            contract(real_part, cosine) - contract(imag_part, sine_part),
            contract(real_part, sine_part) + contract(imag_part, cosine),
        ]
    )


def body(point_spots, point_values, dest_brick, dest_tile, live_count):
    bricks = lax.axis_size("brick")
    slab_count = lax.axis_size("gz")
    blocks = point_spots.shape[1]
    slot_width = point_spots.shape[3]
    per_dest = max(2, 3 * blocks // (2 * bricks))
    slot_count = bricks * per_dest
    target = dest_brick[0, :, 0]
    block_order = jnp.arange(blocks, dtype=jnp.int32)
    before = (block_order[None, :] < block_order[:, None]) & (target[None, :] == target[:, None])
    slot_index = target * per_dest + jnp.sum(before.astype(jnp.int32), axis=1)
    header = jnp.stack([dest_tile[0], live_count[0]], axis=1)
    spots_out = (
        jnp.zeros((slot_count, 3, slot_width), jnp.float32).at[slot_index].set(point_spots[0])
    )
    values_out = (
        jnp.zeros((slot_count, 2, slot_width), jnp.float32).at[slot_index].set(point_values[0])
    )
    header_out = jnp.zeros((slot_count, 2), jnp.int32).at[slot_index].set(header)
    spots_in, values_in, header_in = (
        lax.all_to_all(spots_out, "brick", split_axis=0, concat_axis=0, tiled=True),
        lax.all_to_all(values_out, "brick", split_axis=0, concat_axis=0, tiled=True),
        lax.all_to_all(header_out, "brick", split_axis=0, concat_axis=0, tiled=True),
    )
    brick_x = GRID // (bricks // 4)
    brick_y = GRID // 4
    brick_z = GRID // slab_count
    tiles_x = brick_x // TX
    tiles_z = brick_z // TZ
    group_size = math.gcd(slot_count, 64)
    cells_x = jnp.arange(TX, dtype=jnp.float32)
    cells_y = jnp.arange(brick_y, dtype=jnp.float32)
    cells_z = jnp.arange(TZ, dtype=jnp.float32)

    def spread(grid_sum, turn_index):
        first_row = turn_index * group_size
        spot_rows = lax.dynamic_slice_in_dim(spots_in, first_row, group_size, 0)
        value_rows = lax.dynamic_slice_in_dim(values_in, first_row, group_size, 0)
        head_rows = lax.dynamic_slice_in_dim(header_in, first_row, group_size, 0)
        pos_x = -1.0 + (TX + 2) * spot_rows[:, 0, :]
        pos_y = -1.0 + (brick_y + 2) * spot_rows[:, 1, :]
        pos_z = -1.0 + (TZ + 2) * spot_rows[:, 2, :]
        weight_x = kernel(cells_x[None, None, :] - pos_x[:, :, None]).astype(jnp.bfloat16)
        weight_y = kernel(cells_y[None, None, :] - pos_y[:, :, None])
        weight_z = kernel(cells_z[None, None, :] - pos_z[:, :, None])
        live_mask = jnp.arange(slot_width, dtype=jnp.int32)[None, :] < head_rows[:, 1:2]
        amplitude = jnp.where(live_mask[:, None, :], value_rows, 0.0)
        yz_plane = weight_z[:, :, :, None] * weight_y[:, :, None, :]
        yz_terms = (amplitude[:, :, :, None, None] * yz_plane[:, None]).astype(jnp.bfloat16)
        yz_terms = yz_terms.reshape(group_size, 2, slot_width, TZ * brick_y)
        pieces = jnp.einsum(
            "scj,sack->sajk", weight_x, yz_terms, preferred_element_type=jnp.float32
        )
        return (grid_sum.at[head_rows[:, 0]].add(pieces), None)

    grid_sum = jnp.zeros((tiles_x * tiles_z, 2, TX, TZ * brick_y), jnp.float32)
    grid_sum, _ = lax.scan(spread, grid_sum, jnp.arange(slot_count // group_size))
    cosine, sine_part = tables(GRID)
    z_cos = cosine.reshape(GRID // TZ, TZ, GRID)
    z_sin = sine_part.reshape(GRID // TZ, TZ, GRID)
    blocked = grid_sum.reshape(tiles_x, tiles_z, 2, TX, TZ, brick_y)
    piece = lax.all_to_all(blocked, "gz", split_axis=0, concat_axis=1, tiled=True)
    pencil = rotate("panby,abk->kpny", piece[:, :, 0], piece[:, :, 1], z_cos, z_sin)
    column_width = brick_x // slab_count
    pencil = pencil.reshape(2, GRID, column_width, brick_y)
    x_cos = cosine.reshape(bricks // 4, slab_count, column_width, GRID)
    x_sin = sine_part.reshape(bricks // 4, slab_count, column_width, GRID)
    piece = lax.all_to_all(pencil, ("brick", "gz"), split_axis=1, concat_axis=2, tiled=True)
    z_depth = piece.shape[1]
    item_count = piece.shape[3]
    shaped = piece.reshape(2, z_depth, bricks // 4, 4, slab_count, column_width, item_count)
    einsum_form = "zbqgwn,bgwk->zkqn"
    planes = rotate(einsum_form, shaped[0], shaped[1], x_cos, x_sin)
    y_cos = cosine.reshape(4, brick_y, GRID)
    y_sin = sine_part.reshape(4, brick_y, GRID)
    density = rotate("zkqy,qyl->zkl", planes[0], planes[1], y_cos, y_sin)
    z_depth = density.shape[1]
    corrections = correction(GRID)
    flat_rank = lax.axis_index(("brick", "gz"))
    z_corr = lax.dynamic_slice_in_dim(corrections, flat_rank * z_depth, z_depth, 0)
    unit_scale = GRID ** (-1.5)
    return (
        density
        * unit_scale
        / (
            z_corr[None, :, None, None]
            * corrections[None, None, :, None]
            * corrections[None, None, None, :]
        )
    )


def solution(mesh):
    in_specs = (
        P("gz", "brick", None, None),
        P("gz", "brick", None, None),
        P("gz", "brick", None),
        P("gz", "brick"),
        P("gz", "brick"),
    )
    out_specs = P(None, ("brick", "gz"), None, None)
    return jax.shard_map(body, mesh=mesh, in_specs=in_specs, out_specs=out_specs, check_vma=False)
```

profile of v0, /device:TPU:90, one launch (start us, length us, event | category | flops | bytes accessed | tf_op | source)
XLA Modules:
  0.0 841.3 jit_solution(17982688312330912489)
XLA Ops:
  14.0 25.9 %scatter_fusion.2 = f32[384,3,128]{2,1,0:T(4,128)} fusion(f32[384,3,128]{2,1,0:T(4,128)} %broadcast_in_dim.19, s32[256]{0:T(256)S(1)} %bitcast.190, f32[256,3,128]{2,1,0:T(4,128)S(1)} %copy.70), kind=kCustom, calls=%fused_computation.3 | custom fusion | bytes 1180672 | tf_op jit(solution)/shard_map/scatter | solution.py:69
  47.9 24.1 %scatter_fusion.1 = f32[384,2,128]{2,1,0:T(2,128)} fusion(f32[384,2,128]{2,1,0:T(2,128)} %broadcast_in_dim.18, s32[256]{0:T(256)S(1)} %bitcast.191, f32[256,2,128]{2,1,0:T(2,128)S(1)} %bitcast.187), kind=kCustom, calls=%fused_computation.2 | custom fusion | bytes 787456 | tf_op jit(solution)/shard_map/scatter | solution.py:72
  89.5 358.3 %while.11 = (s32[]{:T(128)}, f32[128,2,16,512]{3,2,1,0:T(8,128)}, s32[6]{0:T(128)S(1)}, s32[384,2]{0,1:T(2,128)S(1)}, f32[384,2,128]{2,1,0:T(2,128)S(1)}, /*inde...) while((s32[]{:T(128)}, f32[128,2,16,512]{3,2,1,0:T(8,128)}, ...), condition=%wide.region_6.7_spmd.clone, body=%wide.region_4.6_spmd.clone.sunk | while | flops 301572288 | bytes 93833976 | solution.py:112
  95.7 10.9 %broadcast_multiply_fusion.5 = f32[64,128,4,128]{3,2,1,0:T(4,128)} fusion(f32[64,128,128]{2,1,0:T(8,128)S(1)} %fusion.187, f32[64,128,4]{2,1,0:T(8,128)S(1)} %copy-done), kind=kLoop, calls=%fused_computation.11.clone.1 | loop fusion | flops 4194304 | bytes 21102592 | tf_op jit(solution)/shard_map/while/body/eval_jaxpr/mul | solution.py:103
  106.6 19.9 %mul.1247 = f32[64,128,512]{2,1,0:T(8,128)} reshape(f32[64,128,4,128]{3,2,1,0:T(4,128)} %broadcast_multiply_fusion.5) | data formatting | bytes 33554432 | tf_op jit(solution)/shard_map/while/body/eval_jaxpr/mul | solution.py:103
  135.6 13.4 %scatter_fusion = f32[128,2,16,512]{3,2,1,0:T(8,128)} fusion(f32[128,2,16,512]{3,2,1,0:T(8,128)} %get-tuple-element.184, s32[64]{0:T(128)S(1)} %get-tuple-element.166, f32[64,2,16,512]{3,2,1,0:T(8,128)} %fusion.189), kind=kCustom, calls=%fused_computation.clone.clone.1 | custom fusion | flops 1048576 | bytes 12583168 | tf_op jit(solution)/shard_map/while/body/eval_jaxpr/scatter-add | solution.py:109
  155.2 10.9 %broadcast_multiply_fusion.5 = f32[64,128,4,128]{3,2,1,0:T(4,128)} fusion(f32[64,128,128]{2,1,0:T(8,128)S(1)} %fusion.187, f32[64,128,4]{2,1,0:T(8,128)S(1)} %copy-done), kind=kLoop, calls=%fused_computation.11.clone.1 | loop fusion | flops 4194304 | bytes 21102592 | tf_op jit(solution)/shard_map/while/body/eval_jaxpr/mul | solution.py:103
  166.1 19.9 %mul.1247 = f32[64,128,512]{2,1,0:T(8,128)} reshape(f32[64,128,4,128]{3,2,1,0:T(4,128)} %broadcast_multiply_fusion.5) | data formatting | bytes 33554432 | tf_op jit(solution)/shard_map/while/body/eval_jaxpr/mul | solution.py:103
  195.0 13.9 %scatter_fusion = f32[128,2,16,512]{3,2,1,0:T(8,128)} fusion(f32[128,2,16,512]{3,2,1,0:T(8,128)} %get-tuple-element.184, s32[64]{0:T(128)S(1)} %get-tuple-element.166, f32[64,2,16,512]{3,2,1,0:T(8,128)} %fusion.189), kind=kCustom, calls=%fused_computation.clone.clone.1 | custom fusion | flops 1048576 | bytes 12583168 | tf_op jit(solution)/shard_map/while/body/eval_jaxpr/scatter-add | solution.py:109
  215.1 10.9 %broadcast_multiply_fusion.5 = f32[64,128,4,128]{3,2,1,0:T(4,128)} fusion(f32[64,128,128]{2,1,0:T(8,128)S(1)} %fusion.187, f32[64,128,4]{2,1,0:T(8,128)S(1)} %copy-done), kind=kLoop, calls=%fused_computation.11.clone.1 | loop fusion | flops 4194304 | bytes 21102592 | tf_op jit(solution)/shard_map/while/body/eval_jaxpr/mul | solution.py:103
  226.0 19.9 %mul.1247 = f32[64,128,512]{2,1,0:T(8,128)} reshape(f32[64,128,4,128]{3,2,1,0:T(4,128)} %broadcast_multiply_fusion.5) | data formatting | bytes 33554432 | tf_op jit(solution)/shard_map/while/body/eval_jaxpr/mul | solution.py:103
  254.9 14.0 %scatter_fusion = f32[128,2,16,512]{3,2,1,0:T(8,128)} fusion(f32[128,2,16,512]{3,2,1,0:T(8,128)} %get-tuple-element.184, s32[64]{0:T(128)S(1)} %get-tuple-element.166, f32[64,2,16,512]{3,2,1,0:T(8,128)} %fusion.189), kind=kCustom, calls=%fused_computation.clone.clone.1 | custom fusion | flops 1048576 | bytes 12583168 | tf_op jit(solution)/shard_map/while/body/eval_jaxpr/scatter-add | solution.py:109
  275.1 10.9 %broadcast_multiply_fusion.5 = f32[64,128,4,128]{3,2,1,0:T(4,128)} fusion(f32[64,128,128]{2,1,0:T(8,128)S(1)} %fusion.187, f32[64,128,4]{2,1,0:T(8,128)S(1)} %copy-done), kind=kLoop, calls=%fused_computation.11.clone.1 | loop fusion | flops 4194304 | bytes 21102592 | tf_op jit(solution)/shard_map/while/body/eval_jaxpr/mul | solution.py:103
  286.0 19.9 %mul.1247 = f32[64,128,512]{2,1,0:T(8,128)} reshape(f32[64,128,4,128]{3,2,1,0:T(4,128)} %broadcast_multiply_fusion.5) | data formatting | bytes 33554432 | tf_op jit(solution)/shard_map/while/body/eval_jaxpr/mul | solution.py:103
  315.0 13.3 %scatter_fusion = f32[128,2,16,512]{3,2,1,0:T(8,128)} fusion(f32[128,2,16,512]{3,2,1,0:T(8,128)} %get-tuple-element.184, s32[64]{0:T(128)S(1)} %get-tuple-element.166, f32[64,2,16,512]{3,2,1,0:T(8,128)} %fusion.189), kind=kCustom, calls=%fused_computation.clone.clone.1 | custom fusion | flops 1048576 | bytes 12583168 | tf_op jit(solution)/shard_map/while/body/eval_jaxpr/scatter-add | solution.py:109
  345.4 19.9 %mul.1247 = f32[64,128,512]{2,1,0:T(8,128)} reshape(f32[64,128,4,128]{3,2,1,0:T(4,128)} %broadcast_multiply_fusion.5) | data formatting | bytes 33554432 | tf_op jit(solution)/shard_map/while/body/eval_jaxpr/mul | solution.py:103
  374.3 13.6 %scatter_fusion = f32[128,2,16,512]{3,2,1,0:T(8,128)} fusion(f32[128,2,16,512]{3,2,1,0:T(8,128)} %get-tuple-element.184, s32[64]{0:T(128)S(1)} %get-tuple-element.166, f32[64,2,16,512]{3,2,1,0:T(8,128)} %fusion.189), kind=kCustom, calls=%fused_computation.clone.clone.1 | custom fusion | flops 1048576 | bytes 12583168 | tf_op jit(solution)/shard_map/while/body/eval_jaxpr/scatter-add | solution.py:109
  405.0 19.9 %mul.1247 = f32[64,128,512]{2,1,0:T(8,128)} reshape(f32[64,128,4,128]{3,2,1,0:T(4,128)} %broadcast_multiply_fusion.5) | data formatting | bytes 33554432 | tf_op jit(solution)/shard_map/while/body/eval_jaxpr/mul | solution.py:103
  433.9 13.9 %scatter_fusion = f32[128,2,16,512]{3,2,1,0:T(8,128)} fusion(f32[128,2,16,512]{3,2,1,0:T(8,128)} %get-tuple-element.184, s32[64]{0:T(128)S(1)} %get-tuple-element.166, f32[64,2,16,512]{3,2,1,0:T(8,128)} %fusion.189), kind=kCustom, calls=%fused_computation.clone.clone.1 | custom fusion | flops 1048576 | bytes 12583168 | tf_op jit(solution)/shard_map/while/body/eval_jaxpr/scatter-add | solution.py:109
  457.7 13.3 %copy.72 = f32[8,16,2,16,4,128]{5,1,4,3,2,0:T(8,128)} copy(f32[8,16,2,16,4,128]{5,4,3,2,1,0:T(4,128)} %reshape.431) | data formatting | bytes 16777216 | tf_op jit(solution)/shard_map/reshape | solution.py:116
  476.8 93.1 %all-to-all-done.3 = f32[8,16,2,16,4,128]{5,1,4,3,2,0:T(8,128)} async-done(((f32[8,16,2,16,4,128]{5,1,4,3,2,0:T(8,128)}), f32[8,16,2,16,4,128]{5,1,4,3,2,0:T(8,128)}, u32[]{:S(2)}, u32[]{:S(2)}) %all-to-all-start.3) | async-done | bytes 8388640 | tf_op jit(solution)/shard_map/all_to_all | solution.py:117
  585.2 11.3 %fusion.58 = f32[512,16,128,1]{2,0,3,1:T(8,128)S(1)} fusion(f32[1,128,2,16,4,128]{5,1,4,3,2,0:T(8,128)S(1)} %bitcast.177, s32[128,4]{0,1:T(4,128)S(1)} %multiply_add_fusion.2), kind=kOutput, calls=%fused_computation.81 | convolution fusion | flops 6446120960 | bytes 8390656 | tf_op jit(solution)/shard_map/panby,abk->kpny/dot_general | solution.py:40
  596.5 11.5 %fusion.57 = f32[1,512,1,16,128]{4,1,3,2,0:T(8,128)S(1)} fusion(f32[512,16,128,1]{2,0,3,1:T(8,128)S(1)} %fusion.59, f32[1,128,2,16,4,128]{5,1,4,3,2,0:T(8,128)S(1)} %bitcast.178, s32[128,4]{0,1:T(4,128)S(1)} %multiply_add_fusion.2), kind=kOutput, calls=%fused_computation.80 | convolution fusion | flops 6447169536 | bytes 12584960 | tf_op jit(solution)/shard_map/panby,abk->kpny/dot_general | solution.py:40
  608.1 11.6 %fusion.56 = f32[1,512,1,16,128]{4,1,3,2,0:T(8,128)S(1)} fusion(f32[512,16,128,1]{2,0,3,1:T(8,128)S(1)} %fusion.58, f32[1,128,2,16,4,128]{5,1,4,3,2,0:T(8,128)S(1)} %bitcast.179, s32[128,4]{0,1:T(4,128)S(1)} %multiply_add_fusion.2), kind=kOutput, calls=%fused_computation.78 | convolution fusion | flops 6447169536 | bytes 12584960 | tf_op jit(solution)/shard_map/panby,abk->kpny/dot_general | solution.py:40
  641.8 99.8 %all-to-all-done.4 = f32[2,512,16,128]{3,2,0,1:T(8,128)} async-done(((f32[2,512,16,128]{3,2,0,1:T(8,128)}), f32[2,512,16,128]{3,2,0,1:T(8,128)}, u32[]{:S(2)}, u32[]{:S(2)}) %all-to-all-start.4) | async-done | bytes 8388640 | tf_op jit(solution)/shard_map/all_to_all | solution.py:123
  747.2 11.0 %fusion.62 = f32[512,4,4,128,1,1]{3,0,5,4,2,1:T(8,128)S(1)} fusion(f32[4,4,4,8,16,128]{5,4,0,3,2,1:T(8,128)S(1)} %bitcast.183, s32[4,8,16]{2,1,0:T(8,128)S(1)} %multiply_add_fusion), kind=kOutput, calls=%fused_computation.85 | convolution fusion | flops 6446120960 | bytes 8390656 | tf_op jit(solution)/shard_map/zbqgwn,bgwk->zkqn/dot_general | solution.py:40
  758.2 11.0 %fusion.64 = f32[512,4,4,128,1,1]{3,0,5,4,2,1:T(8,128)S(1)} fusion(f32[4,4,4,8,16,128]{5,4,0,3,2,1:T(8,128)S(1)} %bitcast.184, s32[4,8,16]{2,1,0:T(8,128)S(1)} %multiply_add_fusion), kind=kOutput, calls=%fused_computation.87 | convolution fusion | flops 6446120960 | bytes 8390656 | tf_op jit(solution)/shard_map/zbqgwn,bgwk->zkqn/dot_general | solution.py:40
  780.0 11.5 %fusion.91 = f32[4,512,512,1]{2,1,3,0:T(8,128)S(1)} fusion(f32[4,512,4,128]{3,1,2,0:T(8,128)S(1)} %fusion.53, s32[4,128]{1,0:T(4,128)S(1)} %multiply_add_fusion.1), kind=kOutput, calls=%fused_computation.120 | convolution fusion | flops 6446120960 | bytes 8390656 | tf_op jit(solution)/shard_map/zkqy,qyl->zkl/dot_general | solution.py:40
  791.6 11.3 %fusion.83 = f32[4,512,512,1]{2,1,3,0:T(8,128)S(1)} fusion(f32[4,512,4,128]{3,1,2,0:T(8,128)S(1)} %fusion.53, s32[4,128]{1,0:T(4,128)S(1)} %multiply_add_fusion.1), kind=kOutput, calls=%fused_computation.112 | convolution fusion | flops 6446120960 | bytes 8390656 | tf_op jit(solution)/shard_map/zkqy,qyl->zkl/dot_general | solution.py:40
  802.9 11.0 %fusion.52 = f32[4,512,4,128]{3,1,2,0:T(8,128)S(1)} fusion(f32[512,4,4,128,1,1]{3,0,5,4,2,1:T(8,128)S(1)} %fusion.62, f32[4,4,4,8,16,128]{5,4,0,3,2,1:T(8,128)S(1)} %bitcast.182, s32[4,8,16]{2,1,0:T(8,128)S(1)} %multiply_add_fusion), kind=kOutput, calls=%fused_computation.70 | convolution fusion | flops 6447169536 | bytes 12584960 | tf_op jit(solution)/shard_map/zbqgwn,bgwk->zkqn/dot_general | solution.py:40
  813.9 11.6 %fusion.55 = f32[1,4,512,512]{3,2,1,0:T(8,128)S(1)} fusion(f32[4,512,512,1]{2,1,3,0:T(8,128)S(1)} %fusion.91, f32[4,512,4,128]{3,1,2,0:T(8,128)S(1)} %fusion.52, s32[4,128]{1,0:T(4,128)S(1)} %multiply_add_fusion.1), kind=kOutput, calls=%fused_computation.76 | convolution fusion | flops 6447169536 | bytes 12584960 | tf_op jit(solution)/shard_map/zkqy,qyl->zkl/dot_general | solution.py:40
  825.5 11.4 %fusion.54 = f32[1,4,512,512]{3,2,1,0:T(8,128)S(1)} fusion(f32[4,512,512,1]{2,1,3,0:T(8,128)S(1)} %fusion.83, f32[4,512,4,128]{3,1,2,0:T(8,128)S(1)} %fusion.52, s32[4,128]{1,0:T(4,128)S(1)} %multiply_add_fusion.1), kind=kOutput, calls=%fused_computation.74 | convolution fusion | flops 6447169536 | bytes 12584960 | tf_op jit(solution)/shard_map/zkqy,qyl->zkl/dot_general | solution.py:40
  (120 shorter events, 222.2 us)
Async XLA Ops:
  0.0 47.9 %copy-start.2 = (f32[1,256,2,128]{3,2,1,0:T(2,128)S(1)}, f32[1,256,2,128]{3,2,1,0:T(2,128)}, u32[]{:S(2)}) copy-start(f32[1,256,2,128]{3,2,1,0:T(2,128)} %param.8) | copy-start | bytes 786436
  4.5 35.4 %all-to-all-start = ((s32[16,24,2]{1,2,0:T(2,128)}), s32[16,24,2]{1,2,0:T(2,128)S(1)}, u32[]{:S(2)}, u32[]{:S(2)}) async-start(s32[16,24,2]{1,2,0:T(2,128)} %copy.68), calls=%async_computation | async-start | bytes 32768 | tf_op jit(solution)/shard_map/all_to_all | solution.py:78
  39.9 32.2 %all-to-all-start.2 = ((f32[384,3,128]{2,1,0:T(4,128)}), f32[384,3,128]{2,1,0:T(4,128)S(1)}, u32[]{:S(2)}, u32[]{:S(2)}) async-start(f32[384,3,128]{2,1,0:T(4,128)} %scatter_fusion.2), calls=%async_computation.2 | async-start | bytes 1572864 | tf_op jit(solution)/shard_map/all_to_all | solution.py:76
  72.0 13.0 %all-to-all-start.1 = ((f32[384,2,128]{2,1,0:T(2,128)}), f32[384,2,128]{2,1,0:T(2,128)S(1)}, u32[]{:S(2)}, u32[]{:S(2)}) async-start(f32[384,2,128]{2,1,0:T(2,128)} %scatter_fusion.1), calls=%async_computation.1 | async-start | bytes 786432 | tf_op jit(solution)/shard_map/all_to_all | solution.py:77
  93.5 2.2 copy-start
  153.0 2.2 copy-start
  212.9 2.2 copy-start
  272.9 2.2 copy-start
  332.3 2.2 copy-start
  391.9 2.2 copy-start
  471.1 98.8 %all-to-all-start.3 = ((f32[8,16,2,16,4,128]{5,1,4,3,2,0:T(8,128)}), f32[8,16,2,16,4,128]{5,1,4,3,2,0:T(8,128)}, u32[]{:S(2)}, u32[]{:S(2)}) async-start(f32[8,16,2,16,4,128]{5,1,4,3,2,0:T(8,128)} %copy.72), calls=%async_computation.3 | async-start | bytes 16777216 | tf_op jit(solution)/shard_map/all_to_all | solution.py:117
  628.8 112.8 %all-to-all-start.4 = ((f32[2,512,16,128]{3,2,0,1:T(8,128)}), f32[2,512,16,128]{3,2,0,1:T(8,128)}, u32[]{:S(2)}, u32[]{:S(2)}) async-start(f32[2,512,16,128]{3,2,0,1:T(8,128)} %copy.74), calls=%async_computation.4 | async-start | bytes 16777216 | tf_op jit(solution)/shard_map/all_to_all | solution.py:123
  825.5 11.4 %copy-start.1 = (f32[4,512,512]{2,1,0:T(8,128)S(1)}, f32[4,512,512]{2,1,0:T(8,128)}, u32[]{:S(2)}) copy-start(f32[4,512,512]{2,1,0:T(8,128)} %broadcast_multiply_fusion.1) | copy-start | bytes 12582916
where the time goes:
time: 850 us; the launch traced here: 841 us
  local copies, waits for them, and re-layouts  245 us (29%)
  waiting for transfers between devices  198 us (23%)
  matrix products  188 us (22%)
  other arithmetic  168 us (20%)
  starting transfers between devices  37.2 us (4%)
    dot_general x12, matrix products, contract(): jnp.einsum(einsum_form, left_side, right_side, precision=lax.Precision.HI...  135 us
    mul x6, local copies, waits for them, and re-layouts, spread(): yz_plane = weight_z[:, :, :, None] * weight_y[:, :, None, :]  119 us
    all_to_all x1, waiting for transfers between devices, body(): lax.all_to_all(pencil, ('brick', 'gz'), split_axis=1, concat_axis=2, tile...  99.8 us
    all_to_all x1, waiting for transfers between devices, body(): lax.all_to_all(blocked, 'gz', split_axis=0, concat_axis=1, tiled=True)  93.1 us
    scatter-add x6, other arithmetic, spread(): return (grid_sum.at[head_rows[:, 0]].add(pieces), None)  82.2 us
    mul x6, other arithmetic, spread(): yz_plane = weight_z[:, :, :, None] * weight_y[:, :, None, :]  65.4 us
    dot_general x6, matrix products, spread(): jnp.einsum('scj,sack->sajk', weight_x, yz_terms, preferred_element_type=j...  52.9 us
    scatter x1, local copies, waits for them, and re-layouts, body(): jnp.zeros((slot_count, 3, slot_width), jnp.float32).at[slot_index]  25.9 us
  transfers between devices with their start and end apart: 5, of which 3 were waited for; matrix products, arithmetic and copies ran while one was open for 7% of the time, Pallas kernels for 0%

commit v1 on v0

v1 whole, which is shorter than its diff:
```python
import functools
import math

import jax
import jax.numpy as jnp
import ml_dtypes
import numpy as np
from jax import lax
from jax.experimental import pallas as pl
from jax.experimental.pallas import tpu as pltpu
from jax.sharding import PartitionSpec as P

GRID = 512
TX = 16
TZ = 4
CAP = 128
AXES = ("brick", "gz")
PER_DEST = 24
ROWS1 = 5 * PER_DEST + 8
ROOM = 80
ROWS2 = 5 * ROOM + 8
LAST = 127
GROUP = 4
VMEM_LIMIT = 56 * 1024 * 1024


def correction_of(length):
    places = np.arange(length)
    shifted = np.where(places < length // 2, places, places - length)
    nodes = np.arange(-63, 64)
    weights = np.maximum(0.0, 1.0 - (nodes / 32.0) ** 2 / 4.0) ** 10
    phases = shifted[:, None] * nodes[None, :] * (2.0 * math.pi / (32.0 * length))
    return np.sum(weights[None, :] * np.cos(phases), axis=1) / 32.0


def split(table):
    high = table.astype(np.float32).astype(ml_dtypes.bfloat16)
    low = (table - high.astype(np.float64)).astype(np.float32).astype(ml_dtypes.bfloat16)
    return high, low


def quarter_tables(scale):
    k, b = np.arange(128)[:, None], np.arange(128)[None, :]
    out = []
    for r in range(4):
        turned = (b * (4 * k + r)) % GRID
        angle = turned * (2.0 * math.pi / GRID)
        gain = scale[4 * np.arange(128) + r][:, None]
        c, s = np.cos(angle) * gain, np.sin(angle) * gain
        out.append(np.block([[c, -s], [s, c]]))
    return split(np.stack(out))


def full_table(scale):
    y, k = np.arange(GRID)[:, None], np.arange(GRID)[None, :]
    angle = (y * k % GRID) * (2.0 * math.pi / GRID)
    c, s = np.cos(angle) * scale[None, :], np.sin(angle) * scale[None, :]
    return np.block([[c, s], [-s, c]]).astype(np.float32).astype(ml_dtypes.bfloat16)


def lanes():
    return lax.broadcasted_iota(jnp.int32, (1, CAP), 1)


def pack_bricks(brick_ref, tile_ref, live_ref, spots_ref, values_ref, out_ref, count_ref):
    lane = lanes()
    for b in range(16):
        count_ref[b] = 0
        out_ref[b * ROWS1 + 5 * PER_DEST : (b + 1) * ROWS1, :] = jnp.zeros((8, CAP), jnp.float32)

    def step(i, tally):
        b = brick_ref[i]
        r = count_ref[b]
        count_ref[b] = r + 1
        base = b * ROWS1
        for d in range(3):
            out_ref[pl.ds(base + d * PER_DEST + r, 1), :] = spots_ref[i, d : d + 1, :]
        live = lane < live_ref[i]
        for d in range(2):
            out_ref[pl.ds(base + (3 + d) * PER_DEST + r, 1), :] = jnp.where(
                live, values_ref[i, d : d + 1, :], 0.0
            )
        head = pl.ds(base + 5 * PER_DEST, 1)
        tile = tile_ref[i]
        out_ref[head, :] = jnp.where(lane == r, tile.astype(jnp.float32), out_ref[head, :])
        key = b * 8 + lax.shift_right_logical(tile, 4)
        return tally + jnp.where(lane == key, 1.0, 0.0)

    tally = lax.fori_loop(0, 256, step, jnp.zeros((1, CAP), jnp.float32), unroll=4)
    for b in range(16):
        row = b * ROWS1 + 5 * PER_DEST
        total = count_ref[b].astype(jnp.float32)
        out_ref[row : row + 1, :] = jnp.where(lane == LAST, total, out_ref[row : row + 1, :])
        out_ref[row + 1 : row + 2, :] = tally


def pack_tiles(round_ref, head_ref, data_ref, out_ref, count_ref):
    lane = lanes()
    first = round_ref[0] * ROOM
    for t in range(8):
        count_ref[t] = 0
        out_ref[t * ROWS2 + 5 * ROOM : (t + 1) * ROWS2, :] = jnp.zeros((8, CAP), jnp.float32)
    spare = 5 * ROOM + 7

    def source(s, carry):
        held = head_ref[s, LAST]

        def step(i, inner):
            tile = head_ref[s, i]
            live = i < held
            tx = lax.shift_right_logical(tile, 4)
            place = count_ref[tx]
            count_ref[tx] = place + live.astype(jnp.int32)
            k = place - first
            good = live & (k >= 0) & (k < ROOM)
            base = tx * ROWS2
            for d in range(5):
                row = jnp.where(good, base + d * ROOM + k, spare)
                out_ref[pl.ds(row, 1), :] = data_ref[pl.ds(s * ROWS1 + d * PER_DEST + i, 1), :]
            head = pl.ds(base + 5 * ROOM, 1)
            depth = (tile & 15).astype(jnp.float32)
            spot = jnp.where(good, k, -1)
            out_ref[head, :] = jnp.where(lane == spot, depth, out_ref[head, :])
            return inner

        return lax.fori_loop(0, PER_DEST, step, carry, unroll=4)

    lax.fori_loop(0, 16, source, 0)
    tally = data_ref[5 * PER_DEST + 1 : 5 * PER_DEST + 2, :]
    for s in range(1, 16):
        row = s * ROWS1 + 5 * PER_DEST + 1
        tally = tally + data_ref[row : row + 1, :]
    for t in range(8):
        row = t * ROWS2 + 5 * ROOM
        count = count_ref[t]
        sent = jnp.clip(count - first, 0, ROOM).astype(jnp.float32)
        out_ref[row : row + 1, :] = jnp.where(lane == LAST, sent, out_ref[row : row + 1, :])
        out_ref[row + 1 : row + 2, :] = tally


def phi10(t):
    square = t * t
    fourth = square * square
    return fourth * fourth * square


def weights_at(cells, position):
    half = cells - 0.5 * position
    return phi10(jnp.maximum(0.0, 1.0 - half * half))


def halves(value):
    high = value.astype(jnp.bfloat16)
    return high, (value - high.astype(jnp.float32)).astype(jnp.bfloat16)


def block_cells(data_ref, row, scale):
    def at(d):
        return data_ref[pl.ds(row + d * ROOM, 1), :]

    pos_x = -1.0 + (TX + 2) * at(0)
    pos_y = -1.0 + (CAP + 2) * at(1)
    pos_z = -1.0 + (TZ + 2) * at(2)
    half_cells = 0.5 * lax.broadcasted_iota(jnp.int32, (CAP, CAP), 0).astype(jnp.float32)
    wy = weights_at(half_cells, pos_y)
    wx = weights_at(half_cells[:TX], pos_x).astype(jnp.bfloat16).astype(jnp.float32)
    wz = weights_at(half_cells[:8], pos_z)
    parts = []
    for d in (3, 4):
        wzv = wz * (at(d) * scale)
        for l in range(TZ):
            parts.append(wx * wzv[l : l + 1, :])
    left = jnp.concatenate(parts, axis=0)
    left_high, left_low = halves(left)
    high, low = halves(wy)
    return lax.dot_general(
        jnp.concatenate([left_high, left_high, left_low], axis=1),
        jnp.concatenate([high, low, high], axis=1),
        (((1,), (1,)), ((), ())),
        preferred_element_type=jnp.float32,
    )


def add_blocks(head_ref, data_ref, grid_ref):
    for g in range(8):
        held = head_ref[g, LAST]

        def group(n, carry, g=g, held=held):
            found = []
            for u in range(GROUP):
                i = n * GROUP + u
                live = i < held
                i = jnp.where(live, i, 0)
                scale = jnp.where(live, 1.0, 0.0).astype(jnp.float32)
                tile = head_ref[g, i] + 16 * g
                found.append((tile, block_cells(data_ref, g * ROWS2 + i, scale)))
            for tile, cells in found:
                for a in range(2):
                    rows = pl.ds(pl.multiple_of(a * 8192 + tile * 64, 64), 64)
                    grid_ref[rows, :] += cells[a * 64 : (a + 1) * 64]
            return carry

        lax.fori_loop(0, (held + GROUP - 1) // GROUP, group, 0)


def start_grid(flag_ref, extra_ref, grid_ref, sem):
    @pl.when(flag_ref[0] > 0)
    def _():
        copy = pltpu.make_async_copy(extra_ref, grid_ref, sem)
        copy.start()
        copy.wait()

    @pl.when(flag_ref[0] <= 0)
    def _():
        def clear(i, carry):
            grid_ref[pl.ds(pl.multiple_of(i * 64, 64), 64), :] = jnp.zeros((64, CAP), jnp.float32)
            return carry

        lax.fori_loop(0, 16384 // 64, clear, 0, unroll=4)


def spread_only(flag_ref, head_ref, data_ref, extra_ref, grid_ref, sem):
    start_grid(flag_ref, extra_ref, grid_ref, sem)
    add_blocks(head_ref, data_ref, grid_ref)


def quarters(re, im):
    s02r, s02i = re[0] + re[2], im[0] + im[2]
    d02r, d02i = re[0] - re[2], im[0] - im[2]
    s13r, s13i = re[1] + re[3], im[1] + im[3]
    d13r, d13i = re[1] - re[3], im[1] - im[3]
    return [
        (s02r + s13r, s02i + s13i),
        (d02r - d13i, d02i + d13r),
        (s02r - s13r, s02i - s13i),
        (d02r + d13i, d02i - d13r),
    ]


def three_pass(high, low, value):
    top, rest = halves(value)

    def dot(a, b):
        return jnp.dot(a, b, preferred_element_type=jnp.float32)

    return dot(high, top) + (dot(high, rest) + dot(low, top))


def spread_and_turn(
    flag_ref, head_ref, data_ref, high_ref, low_ref, extra_ref, out_ref, grid_ref, sem
):
    start_grid(flag_ref, extra_ref, grid_ref, sem)
    add_blocks(head_ref, data_ref, grid_ref)

    def columns(n, carry):
        j = 2 * n

        def plane(a, q):
            return jnp.concatenate(
                [
                    grid_ref[pl.ds(a * 8192 + q * 2048 + j + u, 128, stride=16), :]
                    for u in range(2)
                ],
                axis=1,
            )

        re = [plane(0, q) for q in range(4)]
        im = [plane(1, q) for q in range(4)]
        for r, (real, imag) in enumerate(quarters(re, im)):
            turned = three_pass(high_ref[r], low_ref[r], jnp.concatenate([real, imag], axis=0))
            for a in range(2):
                for u in range(2):
                    out_ref[pl.ds(r * 32 + a * 16 + j + u, 128, stride=128), :] = turned[
                        a * 128 : (a + 1) * 128, u * 128 : (u + 1) * 128
                    ]
        return carry

    lax.fori_loop(0, 8, columns, 0)


def turn_planes(data_ref, high_ref, low_ref, y_ref, out_ref, rows_ref, left_ref):
    def plane(c, bx, by):
        return data_ref[bx, by, :, 0, c].reshape(128, CAP)

    for pair in range(2):
        ys = (2 * pair, 2 * pair + 1)
        re = [jnp.concatenate([plane(0, bx, by) for by in ys], axis=1) for bx in range(4)]
        im = [jnp.concatenate([plane(1, bx, by) for by in ys], axis=1) for bx in range(4)]
        for r, (real, imag) in enumerate(quarters(re, im)):
            turned = three_pass(high_ref[r], low_ref[r], jnp.concatenate([real, imag], axis=0))
            for a in range(2):
                for u in range(2):
                    start = (a * 4 + ys[u]) * GRID + r
                    rows_ref[pl.ds(start, 128, stride=4), :] = turned[
                        a * 128 : (a + 1) * 128, u * 128 : (u + 1) * 128
                    ]
    for n in range(8):
        left_ref[:, n * 128 : (n + 1) * 128] = rows_ref[n * GRID : (n + 1) * GRID, :].astype(
            jnp.bfloat16
        )
    for n in range(4):
        out_ref[n // 2, 0, :, (n % 2) * 256 : (n % 2 + 1) * 256] = jnp.dot(
            left_ref[...], y_ref[:, n * 256 : (n + 1) * 256], preferred_element_type=jnp.float32
        )


def smem():
    return pl.BlockSpec(memory_space=pltpu.SMEM)


def vmem():
    return pl.BlockSpec(memory_space=pltpu.VMEM)


def params():
    return pltpu.CompilerParams(vmem_limit_bytes=VMEM_LIMIT)


def swap(array, axis):
    return lax.all_to_all(array, axis, split_axis=0, concat_axis=0, tiled=True)


def body(z_high, z_low, x_high, x_low, y_table, spots, values, dest_brick, dest_tile, live_count):
    f32 = jnp.float32
    sent = pl.pallas_call(
        pack_bricks,
        out_shape=jax.ShapeDtypeStruct((16 * ROWS1, CAP), f32),
        in_specs=[smem(), smem(), smem(), vmem(), vmem()],
        out_specs=vmem(),
        scratch_shapes=[pltpu.SMEM((16,), jnp.int32)],
        compiler_params=params(),
        name="pack_bricks",
    )(dest_brick.reshape(256), dest_tile[0], live_count[0], spots[0], values[0])
    held = swap(sent.reshape(16, ROWS1, CAP), "brick")
    head = held[:, 5 * PER_DEST].astype(jnp.int32)
    held = held.reshape(16 * ROWS1, CAP)

    def exchange(turn):
        packed = pl.pallas_call(
            pack_tiles,
            out_shape=jax.ShapeDtypeStruct((8 * ROWS2, CAP), f32),
            in_specs=[smem(), smem(), vmem()],
            out_specs=vmem(),
            scratch_shapes=[pltpu.SMEM((8,), jnp.int32)],
            compiler_params=params(),
            name="pack_tiles",
        )(turn, head, held)
        blocks = swap(packed.reshape(8, ROWS2, CAP), "gz")
        return blocks.reshape(8 * ROWS2, CAP), blocks[:, 5 * ROOM : 5 * ROOM + 2].astype(jnp.int32)

    blocks, heads = exchange(jnp.zeros((1,), jnp.int32))
    tiles = heads[:, 0]
    rounds = ((jnp.max(heads[:, 1]) + ROOM - 1) // ROOM).reshape(1)

    nothing = pl.pallas_call(
        lambda out_ref: None,
        out_shape=jax.ShapeDtypeStruct((16384, CAP), f32),
        out_specs=pl.BlockSpec(memory_space=pl.ANY),
        name="nothing",
    )()

    def more(state):
        return state[0][0] < rounds[0]

    def another(state):
        turn, extra = state
        part, part_heads = exchange(turn)
        extra = pl.pallas_call(
            spread_only,
            out_shape=jax.ShapeDtypeStruct((16384, CAP), f32),
            in_specs=[smem(), smem(), vmem(), pl.BlockSpec(memory_space=pl.ANY)],
            out_specs=vmem(),
            scratch_shapes=[pltpu.SemaphoreType.DMA],
            compiler_params=params(),
            name="spread_only",
        )(turn - 1, part_heads[:, 0], part, extra)
        return turn + 1, extra

    _, extra = lax.while_loop(more, another, (jnp.ones((1,), jnp.int32), nothing))

    columns = pl.pallas_call(
        spread_and_turn,
        out_shape=jax.ShapeDtypeStruct((16384, CAP), f32),
        in_specs=[smem(), smem(), vmem(), vmem(), vmem(), pl.BlockSpec(memory_space=pl.ANY)],
        out_specs=vmem(),
        scratch_shapes=[pltpu.VMEM((16384, CAP), f32), pltpu.SemaphoreType.DMA],
        compiler_params=params(),
        name="spread_and_turn",
    )(rounds - 1, tiles, blocks, z_high, z_low, extra)
    planes = swap(columns.reshape(128, 4, 2, TX, CAP), AXES).reshape(4, 4, 8, 4, 2, TX, CAP)
    return pl.pallas_call(
        turn_planes,
        grid=(4,),
        out_shape=jax.ShapeDtypeStruct((2, 4, GRID, GRID), f32),
        in_specs=[
            pl.BlockSpec((4, 4, 8, 1, 2, TX, CAP), lambda q: (0, 0, 0, q, 0, 0, 0)),
            vmem(),
            vmem(),
            vmem(),
        ],
        out_specs=pl.BlockSpec((2, 1, GRID, GRID), lambda q: (0, q, 0, 0)),
        scratch_shapes=[
            pltpu.VMEM((8 * GRID, CAP), f32),
            pltpu.VMEM((GRID, 2 * GRID), jnp.bfloat16),
        ],
        compiler_params=params(),
        name="turn_planes",
    )(planes, x_high, x_low, y_table)


def solution(mesh):
    in_specs = (
        P("gz", "brick", None, None),
        P("gz", "brick", None, None),
        P("gz", "brick", None),
        P("gz", "brick"),
        P("gz", "brick"),
    )
    out_specs = P(None, AXES, None, None)
    inverse = 1.0 / correction_of(GRID)
    z_high, z_low = quarter_tables(inverse * GRID ** (-1.5))
    x_high, x_low = quarter_tables(inverse)
    y_table = full_table(inverse)

    def whole(*args):
        tables = [jnp.asarray(t) for t in (z_high, z_low, x_high, x_low, y_table)]
        return jax.shard_map(
            functools.partial(body),
            mesh=mesh,
            in_specs=(P(),) * 5 + in_specs,
            out_specs=out_specs,
            check_vma=False,
        )(*tables, *args)

    return whole
```

time: 850 us -> 238 us (0.28)
  the two profiles are of different devices: /device:TPU:90 before, /device:TPU:1 now
where the time goes in v1:
time: 238 us
  blocking collectives  148 us (62%)
  Pallas kernels  57.2 us (24%)
  waiting for transfers between devices  21.8 us (9%)
  starting transfers between devices  6.27 us (3%)
    all_to_all x2, blocking collectives, swap(): return lax.all_to_all(array, axis, split_axis=0, concat_axis=0, tiled=True)  148 us
    pallas_call x1, Pallas kernels, body(): pl.pallas_call(spread_and_turn, out_shape=jax.ShapeDtypeStruct((16384, CA...  32.3 us
    all_to_all x1, waiting for transfers between devices, swap(): return lax.all_to_all(array, axis, split_axis=0, concat_axis=0, tiled=True)  21.8 us
    pallas_call x1, Pallas kernels, body(): pl.pallas_call(turn_planes, grid=(4,), out_shape=jax.ShapeDtypeStruct((2,...  13.6 us
    pallas_call x1, Pallas kernels, exchange(): pl.pallas_call(pack_tiles, out_shape=jax.ShapeDtypeStruct((8 * ROWS2, CAP...  7.12 us
    all_to_all x1, starting transfers between devices, swap(): return lax.all_to_all(array, axis, split_axis=0, concat_axis=0, tiled=True)  6.27 us
  transfers between devices with their start and end apart: 1, of which 1 were waited for; matrix products, arithmetic and copies ran while one was open for 0% of the time, Pallas kernels for 0%

profile of v1, /device:TPU:1, one launch (start us, length us, event | category | flops | bytes accessed | tf_op | source)
XLA Modules:
  0.0 237.6 jit_solution(6524382173898742513)
XLA Ops:
  0.0 2.1 copy.35
  2.1 4.2 %pack_bricks.1 = f32[2048,128]{1,0:T(8,128)} custom-call(s32[256]{0:T(256)} %bitcast.40, s32[256]{0:T(256)} %bitcast.41, s32[256]{0:T(256)} %bitcast.42, f32[256,3,128]{2,1,0:T(4,128)} %bitcast.37, f32[256,2,128]{2,1,0:T(2,128)} %bitcast.38), custom_call_target="tpu_custom_call" | custom-call | tf_op jit(solution)/shard_map/pack_bricks/pallas_call | solution.py:325
  6.2 24.7 %all_to_all.23 = f32[16,128,128]{2,1,0:T(8,128)S(1)} all-to-all(f32[16,128,128]{2,1,0:T(8,128)} %bitcast.36), channel_id=1, replica_groups=mesh['brick'=16,'gz'=8] {'brick'}, dimensions={0} | all-to-all | bytes 2097152 | tf_op jit(solution)/shard_map/all_to_all | solution.py:320
  31.0 7.1 %pack_tiles.5 = f32[3264,128]{1,0:T(8,128)} custom-call(s32[1]{0:T(128)} %constant.34.clone.1.round_ref, s32[16,128]{1,0:T(8,128)S(1)} %convert_bitcast_fusion.head_ref, f32[2048,128]{1,0:T(8,128)S(1)} %bitcast.30), custom_call_target="tpu_custom_call" | custom-call | tf_op jit(solution)/shard_map/pack_tiles/pallas_call | solution.py:339
  38.1 6.3 %all-to-all-start.2 = ((f32[8,408,128]{2,1,0:T(8,128)}), f32[8,408,128]{2,1,0:T(8,128)S(1)}, u32[]{:S(2)}, u32[]{:S(2)}) async-start(f32[8,408,128]{2,1,0:T(8,128)} %bitcast.35), calls=%async_computation.2 | async-start | bytes 3342336 | tf_op jit(solution)/shard_map/all_to_all | solution.py:320
  44.4 21.8 %all-to-all-done.2 = f32[8,408,128]{2,1,0:T(8,128)S(1)} async-done(((f32[8,408,128]{2,1,0:T(8,128)}), f32[8,408,128]{2,1,0:T(8,128)S(1)}, u32[]{:S(2)}, u32[]{:S(2)}) %all-to-all-start.2) | async-done | bytes 1671200 | tf_op jit(solution)/shard_map/all_to_all | solution.py:320
  66.1 0.0 copy-start.1
  66.1 1.3 slice_bitcast_fusion
  68.0 0.0 copy-done.1
  68.0 32.3 %spread_and_turn.1 = f32[16384,128]{1,0:T(8,128)} custom-call(s32[1]{0:T(128)} %bitcast.13.flag_ref, s32[8,128]{1,0:T(8,128)} %get-tuple-element.78.head_ref, f32[3264,128]{1,0:T(8,128)} %bitcast.34, bf16[4,256,256]{2,1,0:T(8,128)(2,1)} %constant.42.clone.high_ref, bf16[4,256,256]{2,1,0:T(8,128)(2,1)} %constant.43.clone.low_ref, ...), custom_call_target="tpu_custom_call" | custom-call | tf_op jit(solution)/shard_map/spread_and_turn/pallas_call | solution.py:381
  100.4 123.6 %all_to_all.24 = f32[128,4,2,16,128]{4,3,2,1,0:T(8,128)} all-to-all(f32[128,4,2,16,128]{4,3,2,1,0:T(8,128)} %bitcast.32), channel_id=1, replica_groups=mesh['brick'=16,'gz'=8] {'brick','gz'}, dimensions={0} | all-to-all | bytes 16777216 | tf_op jit(solution)/shard_map/all_to_all | solution.py:320
  224.0 13.6 %turn_planes.1 = f32[2,4,512,512]{3,2,1,0:T(8,128)} custom-call(f32[4,4,8,4,2,16,128]{6,5,4,3,2,1,0:T(8,128)} %bitcast.33, bf16[4,256,256]{2,1,0:T(8,128)(2,1)} %constant.44.clone.high_ref, bf16[4,256,256]{2,1,0:T(8,128)(2,1)} %constant.45.clone.low_ref, bf16[1024,1024]{1,0:T(8,128)(2,1)} %constant.46.clone.y_ref), custom_call_target="tpu_custom_call" | custom-call | tf_op jit(solution)/shard_map/turn_planes/pallas_call | solution.py:391
  (6 shorter events, 0.0 us)
Async XLA Ops:
  38.1 28.0 %all-to-all-start.2 = ((f32[8,408,128]{2,1,0:T(8,128)}), f32[8,408,128]{2,1,0:T(8,128)S(1)}, u32[]{:S(2)}, u32[]{:S(2)}) async-start(f32[8,408,128]{2,1,0:T(8,128)} %bitcast.35), calls=%async_computation.2 | async-start | bytes 3342336 | tf_op jit(solution)/shard_map/all_to_all | solution.py:320
  66.1 1.9 copy-start.1

commit v2 on v1

--- a/solution.py
+++ b/solution.py
@@ -20,7 +20,13 @@
 ROOM = 80
 ROWS2 = 5 * ROOM + 8
 LAST = 127
-GROUP = 4
+SLOTS = 3
+STRAYS = 32
+ROWS_S = 5 * STRAYS + 8
+MARK = 1e30
+GROUP = 16
+DEPTH = 24
+WIDE = 136
 VMEM_LIMIT = 56 * 1024 * 1024
 
 
@@ -62,6 +68,116 @@
     return lax.broadcasted_iota(jnp.int32, (1, CAP), 1)
 
 
+def pack_blocks(
+    me_ref, brick_ref, tile_ref, live_ref, spots_ref, values_ref, out_ref,
+    place_ref, left_ref, count_ref, turn_ref,
+):
+    lane = lanes()
+
+    def clear(k, carry):
+        count_ref[k] = 0
+        out_ref[pl.ds(k * 16 + 15, 1), :] = jnp.full((1, CAP), -1.0, jnp.float32)
+        return carry
+
+    lax.fori_loop(0, 128, clear, 0, unroll=8)
+    for b in range(16):
+        turn_ref[b] = me_ref[0]
+
+    def direct(i, left):
+        key = brick_ref[i] * 8 + lax.shift_right_logical(tile_ref[i], 4)
+        count = count_ref[key]
+        place_ref[i] = key * 16 + count
+        count_ref[key] = jnp.minimum(count + 1, SLOTS)
+        left_ref[left] = i
+        return left + (count >= SLOTS).astype(jnp.int32)
+
+    strays = lax.fori_loop(0, 256, direct, 0, unroll=4)
+
+    def stray(n, carry):
+        i = left_ref[n]
+        b = brick_ref[i]
+        turn = lax.while_loop(
+            lambda p: count_ref[b * 8 + (p & 7)] >= SLOTS, lambda p: p + 1, turn_ref[b]
+        )
+        key = b * 8 + (turn & 7)
+        place_ref[i] = key * 16 + count_ref[key]
+        count_ref[key] = count_ref[key] + 1
+        turn_ref[b] = turn
+        return carry
+
+    lax.fori_loop(0, strays, stray, 0)
+
+    def move(i, carry):
+        row = place_ref[i]
+        slot = row & 15
+        for d in range(3):
+            out_ref[pl.ds(row + d * SLOTS, 1), :] = spots_ref[d, pl.ds(i, 1), :]
+        live = lane < live_ref[i]
+        for d in range(2):
+            out_ref[pl.ds(row + (3 + d) * SLOTS, 1), :] = jnp.where(
+                live, values_ref[i, d : d + 1, :], 0.0
+            )
+        head = pl.ds(row - slot + 15, 1)
+        out_ref[head, :] = jnp.where(lane == slot, tile_ref[i].astype(jnp.float32), out_ref[head, :])
+        return carry
+
+    lax.fori_loop(0, 256, move, 0, unroll=8)
+
+
+def sort_blocks(
+    me_ref, head_ref, data_ref, out_ref, row_ref, tile_ref, note_ref, left_ref, count_ref
+):
+    lane = lanes()
+    me = me_ref[0]
+    for t in range(8):
+        count_ref[t] = 0
+        out_ref[t * ROWS_S + 5 * STRAYS : (t + 1) * ROWS_S, :] = jnp.zeros((8, CAP), jnp.float32)
+
+    def look(source, found):
+        own, strays = found
+        for c in range(SLOTS):
+            tile = head_ref[source * SLOTS + c]
+            tx = lax.shift_right_arithmetic(tile, 4)
+            straight = (tx == me).astype(jnp.int32)
+            row_ref[own] = source * 16 + c
+            tile_ref[own] = (source & 7) * 16 + (tile & 15)
+            own = own + straight
+            left_ref[strays] = source * SLOTS + c
+            strays = strays + (tile >= 0).astype(jnp.int32) - straight
+        return own, strays
+
+    own, strays = lax.fori_loop(0, 128, look, (0, 0), unroll=2)
+
+    def forward(n, carry):
+        entry = left_ref[n]
+        source = entry // SLOTS
+        row = source * 16 + entry - source * SLOTS
+        tile = head_ref[entry]
+        tx = lax.shift_right_logical(tile, 4)
+        k = count_ref[tx]
+        count_ref[tx] = k + 1
+        k = jnp.minimum(k, STRAYS - 1)
+        for d in range(5):
+            out_ref[pl.ds(tx * ROWS_S + d * STRAYS + k, 1), :] = data_ref[
+                pl.ds(row + d * SLOTS, 1), :
+            ]
+        head = pl.ds(tx * ROWS_S + 5 * STRAYS, 1)
+        depth = ((source & 7) * 16 + (tile & 15)).astype(jnp.float32)
+        out_ref[head, :] = jnp.where(lane == k, depth, out_ref[head, :])
+        return carry
+
+    lax.fori_loop(0, strays, forward, 0)
+    most = count_ref[0]
+    for t in range(8):
+        row = t * ROWS_S + 5 * STRAYS
+        count = count_ref[t]
+        most = jnp.maximum(most, count)
+        sent = jnp.minimum(count, STRAYS).astype(jnp.float32)
+        out_ref[row : row + 1, :] = jnp.where(lane == LAST, sent, out_ref[row : row + 1, :])
+    note_ref[0] = own
+    note_ref[1] = (most > STRAYS).astype(jnp.int32)
+
+
 def pack_bricks(brick_ref, tile_ref, live_ref, spots_ref, values_ref, out_ref, count_ref):
     lane = lanes()
     for b in range(16):
@@ -74,7 +190,7 @@
         count_ref[b] = r + 1
         base = b * ROWS1
         for d in range(3):
-            out_ref[pl.ds(base + d * PER_DEST + r, 1), :] = spots_ref[i, d : d + 1, :]
+            out_ref[pl.ds(base + d * PER_DEST + r, 1), :] = spots_ref[d, pl.ds(i, 1), :]
         live = lane < live_ref[i]
         for d in range(2):
             out_ref[pl.ds(base + (3 + d) * PER_DEST + r, 1), :] = jnp.where(
@@ -154,25 +270,32 @@
     return high, (value - high.astype(jnp.float32)).astype(jnp.bfloat16)
 
 
-def block_cells(data_ref, row, scale):
+def block_cells(data_ref, row, step, scale):
     def at(d):
-        return data_ref[pl.ds(row + d * ROOM, 1), :]
+        return data_ref[pl.ds(row + d * step, 1), :]
 
     pos_x = -1.0 + (TX + 2) * at(0)
     pos_y = -1.0 + (CAP + 2) * at(1)
     pos_z = -1.0 + (TZ + 2) * at(2)
-    half_cells = 0.5 * lax.broadcasted_iota(jnp.int32, (CAP, CAP), 0).astype(jnp.float32)
-    wy = weights_at(half_cells, pos_y)
-    wx = weights_at(half_cells[:TX], pos_x).astype(jnp.bfloat16).astype(jnp.float32)
+    half_cells = 0.5 * lax.broadcasted_iota(jnp.int32, (TX, CAP), 0).astype(jnp.float32)
+    wx = weights_at(half_cells, pos_x).astype(jnp.bfloat16).astype(jnp.float32)
     wz = weights_at(half_cells[:8], pos_z)
     parts = []
     for d in (3, 4):
         wzv = wz * (at(d) * scale)
         for l in range(TZ):
             parts.append(wx * wzv[l : l + 1, :])
-    left = jnp.concatenate(parts, axis=0)
-    left_high, left_low = halves(left)
-    high, low = halves(wy)
+    left_high, left_low = halves(jnp.concatenate(parts, axis=0))
+    first = jnp.floor(pos_y) - 1.0
+    near_high, near_low = halves(weights_at(half_cells[:8], pos_y - first))
+    cells = lax.broadcasted_iota(jnp.int32, (CAP, CAP), 0).astype(jnp.float32)
+    place = cells.astype(jnp.bfloat16) - first.astype(jnp.bfloat16)
+    high = jnp.zeros((CAP, CAP), jnp.bfloat16)
+    low = high
+    for k in range(4):
+        here = place == jnp.bfloat16(k)
+        high = jnp.where(here, near_high[k : k + 1, :], high)
+        low = jnp.where(here, near_low[k : k + 1, :], low)
     return lax.dot_general(
         jnp.concatenate([left_high, left_high, left_low], axis=1),
         jnp.concatenate([high, low, high], axis=1),
@@ -181,47 +304,58 @@
     )
 
 
-def add_blocks(head_ref, data_ref, grid_ref):
-    for g in range(8):
-        held = head_ref[g, LAST]
-
-        def group(n, carry, g=g, held=held):
-            found = []
-            for u in range(GROUP):
-                i = n * GROUP + u
-                live = i < held
-                i = jnp.where(live, i, 0)
-                scale = jnp.where(live, 1.0, 0.0).astype(jnp.float32)
-                tile = head_ref[g, i] + 16 * g
-                found.append((tile, block_cells(data_ref, g * ROWS2 + i, scale)))
-            for tile, cells in found:
-                for a in range(2):
-                    rows = pl.ds(pl.multiple_of(a * 8192 + tile * 64, 64), 64)
-                    grid_ref[rows, :] += cells[a * 64 : (a + 1) * 64]
-            return carry
-
-        lax.fori_loop(0, (held + GROUP - 1) // GROUP, group, 0)
-
-
-def start_grid(flag_ref, extra_ref, grid_ref, sem):
-    @pl.when(flag_ref[0] > 0)
-    def _():
-        copy = pltpu.make_async_copy(extra_ref, grid_ref, sem)
-        copy.start()
-        copy.wait()
-
-    @pl.when(flag_ref[0] <= 0)
-    def _():
-        def clear(i, carry):
-            grid_ref[pl.ds(pl.multiple_of(i * 64, 64), 64), :] = jnp.zeros((64, CAP), jnp.float32)
-            return carry
-
-        lax.fori_loop(0, 16384 // 64, clear, 0, unroll=4)
-
-
-def spread_only(flag_ref, head_ref, data_ref, extra_ref, grid_ref, sem):
-    start_grid(flag_ref, extra_ref, grid_ref, sem)
-    add_blocks(head_ref, data_ref, grid_ref)
+def add_listed(row_ref, tile_ref, held, step, data_ref, grid_ref, depth):
+    def group(n, carry):
+        found = []
+        for u in range(GROUP):
+            i = n * GROUP + u
+            live = i < held
+            i = jnp.where(live, i, 0)
+            scale = jnp.where(live, 1.0, 0.0).astype(jnp.float32)
+            found.append((tile_ref[i], block_cells(data_ref, row_ref[i], step, scale)))
+        for tile, cells in found:
+            for a in range(2):
+                for l in range(TZ):
+                    start = (a * 512 + tile * TZ + l) * depth
+                    rows = pl.ds(pl.multiple_of(start, 8), TX)
+                    part = (a * TZ + l) * TX
+                    grid_ref[rows, :] += cells[part : part + TX]
+        return carry
+
+    lax.fori_loop(0, (held + GROUP - 1) // GROUP, group, 0)
+
+
+def list_headed(head_ref, row_ref, tile_ref, room, base):
+    def source(g, total):
+        def entry(i, at):
+            row_ref[at] = g * (5 * room + 8) + i
+            tile_ref[at] = head_ref[g, i] + base * g
+            return at + 1
+
+        return lax.fori_loop(0, head_ref[g, LAST], entry, total)
+
+    return lax.fori_loop(0, 8, source, 0)
+
+
+def clear_grid(grid_ref):
+    def clear(i, carry):
+        grid_ref[pl.ds(pl.multiple_of(i * 64, 64), 64), :] = jnp.zeros((64, CAP), jnp.float32)
+        return carry
+
+    lax.fori_loop(0, 16384 // 64, clear, 0, unroll=4)
+
+
+def spread_direct(note_ref, row_ref, tile_ref, data_ref, grid_ref):
+    clear_grid(grid_ref)
+    add_listed(row_ref, tile_ref, note_ref[0], SLOTS, data_ref, grid_ref, TX)
+
+
+def spread_round(head_ref, data_ref, from_ref, grid_ref, row_ref, tile_ref, sem):
+    copy = pltpu.make_async_copy(from_ref, grid_ref, sem)
+    copy.start()
+    copy.wait()
+    held = list_headed(head_ref, row_ref, tile_ref, ROOM, 16)
+    add_listed(row_ref, tile_ref, held, ROOM, data_ref, grid_ref, TX)
 
 
 def quarters(re, im):
@@ -247,10 +381,16 @@
 
 
 def spread_and_turn(
-    flag_ref, head_ref, data_ref, high_ref, low_ref, extra_ref, out_ref, grid_ref, sem
+    note_ref, head_ref, data_ref, high_ref, low_ref, from_ref, out_ref,
+    grid_ref, sent_ref, row_ref, tile_ref, sem, out_sem,
 ):
-    start_grid(flag_ref, extra_ref, grid_ref, sem)
-    add_blocks(head_ref, data_ref, grid_ref)
+    copy = pltpu.make_async_copy(from_ref, grid_ref.at[:, pl.ds(0, TX), :], sem)
+    copy.start()
+    held = list_headed(head_ref, row_ref, tile_ref, STRAYS, 0)
+    copy.wait()
+    flat = grid_ref.reshape(1024 * DEPTH, CAP)
+    sent = sent_ref.reshape(128 * WIDE, CAP)
+    add_listed(row_ref, tile_ref, held, STRAYS, data_ref, flat, DEPTH)
 
     def columns(n, carry):
         j = 2 * n
@@ -258,7 +398,7 @@
         def plane(a, q):
             return jnp.concatenate(
                 [
-                    grid_ref[pl.ds(a * 8192 + q * 2048 + j + u, 128, stride=16), :]
+                    flat[pl.ds((a * 512 + q * 128) * DEPTH + j + u, 128, stride=DEPTH), :]
                     for u in range(2)
                 ],
                 axis=1,
@@ -270,15 +410,37 @@
             turned = three_pass(high_ref[r], low_ref[r], jnp.concatenate([real, imag], axis=0))
             for a in range(2):
                 for u in range(2):
-                    out_ref[pl.ds(r * 32 + a * 16 + j + u, 128, stride=128), :] = turned[
+                    sent[pl.ds(r * 32 + a * 16 + j + u, 128, stride=WIDE), :] = turned[
                         a * 128 : (a + 1) * 128, u * 128 : (u + 1) * 128
                     ]
         return carry
 
-    lax.fori_loop(0, 8, columns, 0)
-
-
-def turn_planes(data_ref, high_ref, low_ref, y_ref, out_ref, rows_ref, left_ref):
+    def outward(n):
+        return pltpu.make_async_copy(sent_ref.at[:, n], out_ref.at[:, n], out_sem.at[n])
+
+    lax.fori_loop(0, 4, columns, 0)
+
+    @pl.when(note_ref[1] > 0)
+    def _():
+        sent[pl.ds(0, 128, stride=WIDE), :] = jnp.full((128, CAP), MARK, jnp.float32)
+
+    for n in range(8):
+        outward(2 * n).start()
+    lax.fori_loop(4, 8, columns, 0)
+    for n in range(8):
+        outward(2 * n + 1).start()
+    for n in range(16):
+        outward(n).wait()
+
+
+def turn_planes(data_ref, high_ref, low_ref, y_ref, out_ref, mark_ref, rows_ref, left_ref):
+    @pl.when(pl.program_id(0) == 0)
+    def _():
+        most = data_ref[0, 0, :, 0, 0, 0]
+        for n in range(1, 16):
+            most = jnp.maximum(most, data_ref[n // 4, n % 4, :, 0, 0, 0])
+        mark_ref[0] = (jnp.max(most) > 0.1 * MARK).astype(jnp.int32)
+
     def plane(c, bx, by):
         return data_ref[bx, by, :, 0, c].reshape(128, CAP)
 
@@ -320,92 +482,157 @@
     return lax.all_to_all(array, axis, split_axis=0, concat_axis=0, tiled=True)
 
 
+def call(kernel, out_shape, in_specs, out_specs, **options):
+    return pl.pallas_call(
+        kernel,
+        out_shape=out_shape,
+        in_specs=in_specs,
+        out_specs=out_specs,
+        compiler_params=params(),
+        name=kernel.__name__,
+        **options,
+    )
+
+
+def anywhere():
+    return pl.BlockSpec(memory_space=pl.ANY)
+
+
+def rows_of(rows):
+    return jax.ShapeDtypeStruct((rows, CAP), jnp.float32)
+
+
+def ints(count):
+    return jax.ShapeDtypeStruct((count,), jnp.int32)
+
+
 def body(z_high, z_low, x_high, x_low, y_table, spots, values, dest_brick, dest_tile, live_count):
-    f32 = jnp.float32
-    sent = pl.pallas_call(
-        pack_bricks,
-        out_shape=jax.ShapeDtypeStruct((16 * ROWS1, CAP), f32),
-        in_specs=[smem(), smem(), smem(), vmem(), vmem()],
-        out_specs=vmem(),
-        scratch_shapes=[pltpu.SMEM((16,), jnp.int32)],
-        compiler_params=params(),
-        name="pack_bricks",
-    )(dest_brick.reshape(256), dest_tile[0], live_count[0], spots[0], values[0])
-    held = swap(sent.reshape(16, ROWS1, CAP), "brick")
-    head = held[:, 5 * PER_DEST].astype(jnp.int32)
-    held = held.reshape(16 * ROWS1, CAP)
-
-    def exchange(turn):
-        packed = pl.pallas_call(
-            pack_tiles,
-            out_shape=jax.ShapeDtypeStruct((8 * ROWS2, CAP), f32),
-            in_specs=[smem(), smem(), vmem()],
-            out_specs=vmem(),
-            scratch_shapes=[pltpu.SMEM((8,), jnp.int32)],
-            compiler_params=params(),
-            name="pack_tiles",
-        )(turn, head, held)
-        blocks = swap(packed.reshape(8, ROWS2, CAP), "gz")
-        return blocks.reshape(8 * ROWS2, CAP), blocks[:, 5 * ROOM : 5 * ROOM + 2].astype(jnp.int32)
-
-    blocks, heads = exchange(jnp.zeros((1,), jnp.int32))
-    tiles = heads[:, 0]
-    rounds = ((jnp.max(heads[:, 1]) + ROOM - 1) // ROOM).reshape(1)
-
-    nothing = pl.pallas_call(
-        lambda out_ref: None,
-        out_shape=jax.ShapeDtypeStruct((16384, CAP), f32),
-        out_specs=pl.BlockSpec(memory_space=pl.ANY),
-        name="nothing",
-    )()
-
-    def more(state):
-        return state[0][0] < rounds[0]
-
-    def another(state):
-        turn, extra = state
-        part, part_heads = exchange(turn)
-        extra = pl.pallas_call(
-            spread_only,
-            out_shape=jax.ShapeDtypeStruct((16384, CAP), f32),
-            in_specs=[smem(), smem(), vmem(), pl.BlockSpec(memory_space=pl.ANY)],
-            out_specs=vmem(),
-            scratch_shapes=[pltpu.SemaphoreType.DMA],
-            compiler_params=params(),
-            name="spread_only",
-        )(turn - 1, part_heads[:, 0], part, extra)
-        return turn + 1, extra
-
-    _, extra = lax.while_loop(more, another, (jnp.ones((1,), jnp.int32), nothing))
-
-    columns = pl.pallas_call(
-        spread_and_turn,
-        out_shape=jax.ShapeDtypeStruct((16384, CAP), f32),
-        in_specs=[smem(), smem(), vmem(), vmem(), vmem(), pl.BlockSpec(memory_space=pl.ANY)],
-        out_specs=vmem(),
-        scratch_shapes=[pltpu.VMEM((16384, CAP), f32), pltpu.SemaphoreType.DMA],
-        compiler_params=params(),
-        name="spread_and_turn",
-    )(rounds - 1, tiles, blocks, z_high, z_low, extra)
-    planes = swap(columns.reshape(128, 4, 2, TX, CAP), AXES).reshape(4, 4, 8, 4, 2, TX, CAP)
-    return pl.pallas_call(
-        turn_planes,
-        grid=(4,),
-        out_shape=jax.ShapeDtypeStruct((2, 4, GRID, GRID), f32),
-        in_specs=[
-            pl.BlockSpec((4, 4, 8, 1, 2, TX, CAP), lambda q: (0, 0, 0, q, 0, 0, 0)),
+    points = (
+        dest_brick.reshape(256),
+        dest_tile[0],
+        live_count[0],
+        spots[0].transpose(1, 0, 2),
+        values[0],
+    )
+
+    def finish(note, heads, data, grid):
+        columns = call(
+            spread_and_turn,
+            jax.ShapeDtypeStruct((128, 16, 8, CAP), jnp.float32),
+            [smem(), smem(), vmem(), vmem(), vmem(), anywhere()],
+            anywhere(),
+            scratch_shapes=[
+                pltpu.VMEM((1024, DEPTH, CAP), jnp.float32),
+                pltpu.VMEM((128, WIDE // 8, 8, CAP), jnp.float32),
+                pltpu.SMEM((8 * STRAYS,), jnp.int32),
+                pltpu.SMEM((8 * STRAYS,), jnp.int32),
+                pltpu.SemaphoreType.DMA,
+                pltpu.SemaphoreType.DMA((16,)),
+            ],
+        )(note, heads, data, z_high, z_low, grid.reshape(1024, TX, CAP))
+        planes = swap(columns.reshape(128, 4, 2, TX, CAP), AXES).reshape(4, 4, 8, 4, 2, TX, CAP)
+        return call(
+            turn_planes,
+            (jax.ShapeDtypeStruct((2, 4, GRID, GRID), jnp.float32), ints(1)),
+            [
+                pl.BlockSpec((4, 4, 8, 1, 2, TX, CAP), lambda q: (0, 0, 0, q, 0, 0, 0)),
+                vmem(),
+                vmem(),
+                vmem(),
+            ],
+            (pl.BlockSpec((2, 1, GRID, GRID), lambda q: (0, q, 0, 0)), smem()),
+            grid=(4,),
+            scratch_shapes=[
+                pltpu.VMEM((8 * GRID, CAP), jnp.float32),
+                pltpu.VMEM((GRID, 2 * GRID), jnp.bfloat16),
+            ],
+        )(planes, x_high, x_low, y_table)
+
+    me = lax.axis_index("gz").astype(jnp.int32).reshape(1)
+    sent = call(
+        pack_blocks,
+        rows_of(128 * 16),
+        [smem()] * 4 + [vmem()] * 2,
+        vmem(),
+        scratch_shapes=[pltpu.SMEM((n,), jnp.int32) for n in (256, 264, 128, 16)],
+    )(me, *points)
+    held = swap(sent.reshape(128, 16, CAP), AXES)
+    heads = held[:, 15, :SLOTS].astype(jnp.int32).reshape(128 * SLOTS)
+    held = held.reshape(128 * 16, CAP)
+    strays, rows, tiles, note = call(
+        sort_blocks,
+        (rows_of(8 * ROWS_S), ints(392), ints(392), ints(2)),
+        [smem(), smem(), vmem()],
+        (vmem(), smem(), smem(), smem()),
+        scratch_shapes=[pltpu.SMEM((392,), jnp.int32), pltpu.SMEM((8,), jnp.int32)],
+    )(me, heads, held)
+    strays = swap(strays.reshape(8, ROWS_S, CAP), "gz")
+    grid = call(
+        spread_direct,
+        rows_of(16384),
+        [smem(), smem(), smem(), vmem()],
+        vmem(),
+        cost_estimate=pl.CostEstimate(flops=3 * 10**10, bytes_accessed=10**8, transcendentals=0),
+    )(note, rows, tiles, held)
+    stray_heads = strays[:, 5 * STRAYS].astype(jnp.int32)
+    density, mark = finish(note, stray_heads, strays.reshape(8 * ROWS_S, CAP), grid)
+
+    def general(state):
+        _, again, *given = lax.optimization_barrier((*state, *points))
+        parts = call(
+            pack_bricks,
+            rows_of(16 * ROWS1),
+            [smem()] * 3 + [vmem()] * 2,
             vmem(),
-            vmem(),
-            vmem(),
-        ],
-        out_specs=pl.BlockSpec((2, 1, GRID, GRID), lambda q: (0, q, 0, 0)),
-        scratch_shapes=[
-            pltpu.VMEM((8 * GRID, CAP), f32),
-            pltpu.VMEM((GRID, 2 * GRID), jnp.bfloat16),
-        ],
-        compiler_params=params(),
-        name="turn_planes",
-    )(planes, x_high, x_low, y_table)
+            scratch_shapes=[pltpu.SMEM((16,), jnp.int32)],
+        )(*given)
+        parts = swap(parts.reshape(16, ROWS1, CAP), "brick")
+        head = parts[:, 5 * PER_DEST].astype(jnp.int32)
+        parts = parts.reshape(16 * ROWS1, CAP)
+
+        def another(inner):
+            turn, _, total = inner
+            packed = call(
+                pack_tiles,
+                rows_of(8 * ROWS2),
+                [smem(), smem(), vmem()],
+                vmem(),
+                scratch_shapes=[pltpu.SMEM((8,), jnp.int32)],
+            )(turn, head, parts)
+            blocks = swap(packed.reshape(8, ROWS2, CAP), "gz")
+            told = blocks[:, 5 * ROOM : 5 * ROOM + 2].astype(jnp.int32)
+            total = call(
+                spread_round,
+                rows_of(16384),
+                [smem(), vmem(), anywhere()],
+                vmem(),
+                scratch_shapes=[
+                    pltpu.SMEM((8 * ROOM,), jnp.int32),
+                    pltpu.SMEM((8 * ROOM,), jnp.int32),
+                    pltpu.SemaphoreType.DMA,
+                ],
+            )(told[:, 0], blocks.reshape(8 * ROWS2, CAP), total)
+            return turn + 1, ((jnp.max(told[:, 1]) + ROOM - 1) // ROOM).reshape(1), total
+
+        _, _, total = lax.while_loop(
+            lambda inner: inner[0][0] < inner[1][0],
+            another,
+            (
+                jnp.zeros((1,), jnp.int32),
+                jnp.ones((1,), jnp.int32),
+                jnp.zeros((16384, CAP), jnp.float32),
+            ),
+        )
+        none = jnp.zeros((8, CAP), jnp.int32)
+        return finish(
+            jnp.zeros((2,), jnp.int32),
+            none,
+            jnp.zeros((8 * ROWS_S, CAP), jnp.float32),
+            total,
+        )
+
+    density, _ = lax.while_loop(lambda state: state[1][0] > 0, general, (density, mark))
+    return density
 
 
 def solution(mesh):

time: 238 us -> 212 us (0.89)
  the two profiles are of different devices: /device:TPU:1 before, /device:TPU:90 now
where the time goes in v2:
time: 212 us
  waiting for transfers between devices  104 us (49%)
  Pallas kernels  63.1 us (30%)
  blocking collectives  24.3 us (11%)
  starting transfers between devices  17.6 us (8%)
    all_to_all x2, waiting for transfers between devices, swap(): return lax.all_to_all(array, axis, split_axis=0, concat_axis=0, tiled=True)  104 us
    all_to_all x1, blocking collectives, swap(): return lax.all_to_all(array, axis, split_axis=0, concat_axis=0, tiled=True)  24.3 us
    pallas_call x1, Pallas kernels, body(): call(spread_direct, rows_of(16384), [smem(), smem(), smem(), vmem()], vme...  20.7 us
    all_to_all x2, starting transfers between devices, swap(): return lax.all_to_all(array, axis, split_axis=0, concat_axis=0, tiled=True)  17.6 us
    pallas_call x1, Pallas kernels, finish(): call(spread_and_turn, jax.ShapeDtypeStruct((128, 16, 8, CAP), jnp.float32...  16.8 us
    pallas_call x1, Pallas kernels, finish(): call(turn_planes, (jax.ShapeDtypeStruct((2, 4, GRID, GRID), jnp.float32),...  13 us
    pallas_call x1, Pallas kernels, body(): call(pack_blocks, rows_of(128 * 16), [smem()] * 4 + [vmem()] * 2, vmem(),...  6.65 us
    pallas_call x1, Pallas kernels, body(): call(sort_blocks, (rows_of(8 * ROWS_S), ints(392), ints(392), ints(2)), [...  6.03 us
  transfers between devices with their start and end apart: 2, of which 1 were waited for; matrix products, arithmetic and copies ran while one was open for 0% of the time, Pallas kernels for 10%

profile of v2, /device:TPU:90, one launch (start us, length us, event | category | flops | bytes accessed | tf_op | source)
XLA Modules:
  0.0 211.8 jit_solution(10662705129461589586)
XLA Ops:
  0.0 6.7 %pack_blocks.1 = f32[2048,128]{1,0:T(8,128)} custom-call(s32[1]{0:T(128)} %bitcast.5.me_ref, s32[256]{0:T(256)} %bitcast.70, s32[256]{0:T(256)} %bitcast.72, s32[256]{0:T(256)} %bitcast.74, f32[3,256,128]{2,1,0:T(8,128)} %bitcast.10.spots_ref, f32[256,2,128]{2,1,0:T(2,128)} %bitcast.61), custom_call_target="tpu_custom_call" | custom-call | tf_op jit(solution)/shard_map/pack_blocks/pallas_call | solution.py:552
  6.7 24.3 %all_to_all.51 = f32[128,16,128]{2,1,0:T(8,128)S(1)} all-to-all(f32[128,16,128]{2,1,0:T(8,128)} %bitcast.67), channel_id=1, replica_groups=mesh['brick'=16,'gz'=8] {'brick','gz'}, dimensions={0} | all-to-all | bytes 2097152 | tf_op jit(solution)/shard_map/all_to_all | solution.py:482
  30.9 0.2 fusion
  31.2 0.8 convert_element_type.31.head_ref
  32.0 0.0 copy-done.10
  32.0 6.0 %sort_blocks.1 = (f32[1344,128]{1,0:T(8,128)}, s32[392]{0:T(512)}, s32[392]{0:T(512)}, s32[2]{0:T(128)}) custom-call(s32[1]{0:T(128)} %bitcast.5.me_ref, s32[384]{0:T(512)} %convert_element_type.31.head_ref, f32[2048,128]{1,0:T(8,128)} %bitcast.65), custom_call_target="tpu_custom_call" | custom-call | tf_op jit(solution)/shard_map/sort_blocks/pallas_call | solution.py:562
  38.0 4.7 %all-to-all-start.4 = ((f32[8,168,128]{2,1,0:T(8,128)}), f32[8,168,128]{2,1,0:T(8,128)S(1)}, u32[]{:S(2)}, u32[]{:S(2)}) async-start(f32[8,168,128]{2,1,0:T(8,128)} %bitcast.69), calls=%async_computation.4 | async-start | bytes 1376256 | tf_op jit(solution)/shard_map/all_to_all | solution.py:482
  42.7 20.7 %spread_direct.1 = f32[16384,128]{1,0:T(8,128)} custom-call(s32[2]{0:T(128)} %get-tuple-element.467.note_ref, s32[392]{0:T(512)} %get-tuple-element.469.row_ref, s32[392]{0:T(512)} %get-tuple-element.470.tile_ref, f32[2048,128]{1,0:T(8,128)} %bitcast.66), custom_call_target="tpu_custom_call" | custom-call | flops 30000001024 | bytes 100000000 | tf_op jit(solution)/shard_map/spread_direct/pallas_call | solution.py:570
  63.4 0.0 all-to-all-done.4
  63.4 0.6 convert_bitcast_fusion.head_ref
  64.1 0.3 copy-done.11
  64.4 0.0 copy-done.3
  64.4 0.0 copy-done.5
  64.4 16.8 %spread_and_turn.7 = f32[128,16,8,128]{3,2,1,0:T(8,128)} custom-call(s32[2]{0:T(128)} %get-tuple-element.467.note_ref, s32[8,128]{1,0:T(8,128)} %convert_bitcast_fusion.head_ref, f32[1344,128]{1,0:T(8,128)} %bitcast.68, bf16[4,256,256]{2,1,0:T(8,128)(2,1)S(1)} %copy-done.3, bf16[4,256,256]{2,1,0:T(8,128)(2,1)S(1)} %copy-done.5, f32[1024,16,128]{2,1,0:T(8,128)} %bitcast.63), custom_call_target="tpu_custom_call" | custom-call | tf_op jit(solution)/shard_map/spread_and_turn/pallas_call | solution.py:519
  81.1 0.0 copy-start.1
  81.2 0.0 copy-start.6
  81.2 12.8 %all-to-all-start.5 = ((f32[128,4,2,16,128]{4,3,2,1,0:T(8,128)}), f32[128,4,2,16,128]{4,3,2,1,0:T(8,128)}, u32[]{:S(2)}, u32[]{:S(2)}) async-start(f32[128,4,2,16,128]{4,3,2,1,0:T(8,128)} %bitcast.60), calls=%async_computation.5 | async-start | bytes 16777216 | tf_op jit(solution)/shard_map/all_to_all | solution.py:482
  94.0 0.0 copy-start.4
  94.0 0.0 copy-start.9
  94.0 0.0 copy-start.12
  94.0 0.0 copy-start.13
  94.1 0.0 copy-start.14
  94.1 103.7 %all-to-all-done.5 = f32[128,4,2,16,128]{4,3,2,1,0:T(8,128)} async-done(((f32[128,4,2,16,128]{4,3,2,1,0:T(8,128)}), f32[128,4,2,16,128]{4,3,2,1,0:T(8,128)}, u32[]{:S(2)}, u32[]{:S(2)}) %all-to-all-start.5) | async-done | bytes 8388640 | tf_op jit(solution)/shard_map/all_to_all | solution.py:482
  197.8 0.0 copy-done.1
  197.8 0.0 copy-done.6
  197.8 13.0 %turn_planes.7 = (f32[2,4,512,512]{3,2,1,0:T(8,128)}, s32[1]{0:T(128)}) custom-call(f32[4,4,8,4,2,16,128]{6,5,4,3,2,1,0:T(8,128)} %bitcast.19.data_ref, bf16[4,256,256]{2,1,0:T(8,128)(2,1)S(1)} %copy-done.6, bf16[4,256,256]{2,1,0:T(8,128)(2,1)} %constant.101.clone.low_ref, bf16[1024,1024]{1,0:T(8,128)(2,1)S(1)} %copy-done.1), custom_call_target="tpu_custom_call" | custom-call | tf_op jit(solution)/shard_map/turn_planes/pallas_call | solution.py:534
  210.8 0.0 copy-done.4
  210.8 0.0 copy-done.9
  210.8 0.0 copy-done.12
  210.8 0.0 copy-done.13
  210.8 0.0 copy-done.14
  210.8 0.8 while.43
  (5 shorter events, 0.0 us)
Async XLA Ops:
  30.9 1.0 copy-start.10
  38.0 25.4 %all-to-all-start.4 = ((f32[8,168,128]{2,1,0:T(8,128)}), f32[8,168,128]{2,1,0:T(8,128)S(1)}, u32[]{:S(2)}, u32[]{:S(2)}) async-start(f32[8,168,128]{2,1,0:T(8,128)} %bitcast.69), calls=%async_computation.4 | async-start | bytes 1376256 | tf_op jit(solution)/shard_map/all_to_all | solution.py:482
  42.7 21.7 %copy-start.3 = (bf16[4,256,256]{2,1,0:T(8,128)(2,1)S(1)}, bf16[4,256,256]{2,1,0:T(8,128)(2,1)}, u32[]{:S(2)}) copy-start(bf16[4,256,256]{2,1,0:T(8,128)(2,1)} %constant.98.clone.high_ref) | copy-start | bytes 1572868
  42.7 21.7 %copy-start.5 = (bf16[4,256,256]{2,1,0:T(8,128)(2,1)S(1)}, bf16[4,256,256]{2,1,0:T(8,128)(2,1)}, u32[]{:S(2)}) copy-start(bf16[4,256,256]{2,1,0:T(8,128)(2,1)} %constant.99.clone.low_ref) | copy-start | bytes 1572868
  63.4 0.9 copy-start.11
  81.1 116.6 %copy-start.1 = (bf16[1024,1024]{1,0:T(8,128)(2,1)S(1)}, bf16[1024,1024]{1,0:T(8,128)(2,1)}, u32[]{:S(2)}) copy-start(bf16[1024,1024]{1,0:T(8,128)(2,1)} %constant.102.clone.y_ref) | copy-start | bytes 6291460
  81.2 116.6 %copy-start.6 = (bf16[4,256,256]{2,1,0:T(8,128)(2,1)S(1)}, bf16[4,256,256]{2,1,0:T(8,128)(2,1)}, u32[]{:S(2)}) copy-start(bf16[4,256,256]{2,1,0:T(8,128)(2,1)} %constant.100.clone.high_ref) | copy-start | bytes 1572868
  81.2 116.6 %all-to-all-start.5 = ((f32[128,4,2,16,128]{4,3,2,1,0:T(8,128)}), f32[128,4,2,16,128]{4,3,2,1,0:T(8,128)}, u32[]{:S(2)}, u32[]{:S(2)}) async-start(f32[128,4,2,16,128]{4,3,2,1,0:T(8,128)} %bitcast.60), calls=%async_computation.5 | async-start | bytes 16777216 | tf_op jit(solution)/shard_map/all_to_all | solution.py:482
  94.0 116.7 %copy-start.4 = (bf16[4,256,256]{2,1,0:T(8,128)(2,1)S(1)}, bf16[4,256,256]{2,1,0:T(8,128)(2,1)}, u32[]{:S(2)}) copy-start(bf16[4,256,256]{2,1,0:T(8,128)(2,1)} %constant.98.clone.high_ref) | copy-start | bytes 1572868
  94.0 116.7 %copy-start.9 = (f32[1,256,2,128]{3,2,1,0:T(2,128)S(1)}, f32[1,256,2,128]{3,2,1,0:T(2,128)}, u32[]{:S(2)}) copy-start(f32[1,256,2,128]{3,2,1,0:T(2,128)} %param.15) | copy-start | bytes 786436
  94.0 116.7 %copy-start.12 = (s32[1,256,1]{1,2,0:T(1,128)S(1)}, s32[1,256,1]{1,2,0:T(1,128)}, u32[]{:S(2)}) copy-start(s32[1,256,1]{1,2,0:T(1,128)} %param.16) | copy-start | bytes 3076
  94.0 116.7 %copy-start.13 = (s32[1,256]{1,0:T(1,128)S(1)}, s32[1,256]{1,0:T(1,128)}, u32[]{:S(2)}) copy-start(s32[1,256]{1,0:T(1,128)} %param.17) | copy-start | bytes 3076
  94.1 116.7 %copy-start.14 = (s32[1,256]{1,0:T(1,128)S(1)}, s32[1,256]{1,0:T(1,128)}, u32[]{:S(2)}) copy-start(s32[1,256]{1,0:T(1,128)} %param.18) | copy-start | bytes 3076

commit v3 on v2

--- a/solution.py
+++ b/solution.py
@@ -25,9 +25,17 @@
 ROWS_S = 5 * STRAYS + 8
 MARK = 1e30
 GROUP = 16
+GROUP_LISTED = 32
 DEPTH = 24
 WIDE = 136
-VMEM_LIMIT = 56 * 1024 * 1024
+MIB = 1024 * 1024
+VMEM_MIB = {
+    "pack_blocks": 8,
+    "sort_blocks": 8,
+    "spread_direct": 54,
+    "spread_and_turn": 54,
+    "turn_planes": 28,
+}
 
 
 def correction_of(length):
@@ -133,8 +141,9 @@
         count_ref[t] = 0
         out_ref[t * ROWS_S + 5 * STRAYS : (t + 1) * ROWS_S, :] = jnp.zeros((8, CAP), jnp.float32)
 
-    def look(source, found):
+    def look(n, found):
         own, strays = found
+        source = (n & 15) * 8 + lax.shift_right_logical(n, 4)
         for c in range(SLOTS):
             tile = head_ref[source * SLOTS + c]
             tx = lax.shift_right_arithmetic(tile, 4)
@@ -144,6 +153,7 @@
             own = own + straight
             left_ref[strays] = source * SLOTS + c
             strays = strays + (tile >= 0).astype(jnp.int32) - straight
+        note_ref[2 + lax.shift_right_logical(n, 4)] = own
         return own, strays
 
     own, strays = lax.fori_loop(0, 128, look, (0, 0), unroll=2)
@@ -304,11 +314,11 @@
     )
 
 
-def add_listed(row_ref, tile_ref, held, step, data_ref, grid_ref, depth):
+def add_listed(row_ref, tile_ref, held, step, data_ref, grid_ref, depth, size, after=None):
     def group(n, carry):
         found = []
-        for u in range(GROUP):
-            i = n * GROUP + u
+        for u in range(size):
+            i = n * size + u
             live = i < held
             i = jnp.where(live, i, 0)
             scale = jnp.where(live, 1.0, 0.0).astype(jnp.float32)
@@ -320,9 +330,9 @@
                     rows = pl.ds(pl.multiple_of(start, 8), TX)
                     part = (a * TZ + l) * TX
                     grid_ref[rows, :] += cells[part : part + TX]
-        return carry
-
-    lax.fori_loop(0, (held + GROUP - 1) // GROUP, group, 0)
+        return carry if after is None else after((n + 1) * size, carry)
+
+    return lax.fori_loop(0, (held + size - 1) // size, group, 0)
 
 
 def list_headed(head_ref, row_ref, tile_ref, room, base):
@@ -345,9 +355,31 @@
     lax.fori_loop(0, 16384 // 64, clear, 0, unroll=4)
 
 
-def spread_direct(note_ref, row_ref, tile_ref, data_ref, grid_ref):
+def spread_direct(note_ref, row_ref, tile_ref, data_ref, out_ref, grid_ref, sem):
     clear_grid(grid_ref)
-    add_listed(row_ref, tile_ref, note_ref[0], SLOTS, data_ref, grid_ref, TX)
+
+    def outward(a, slab):
+        rows = pl.ds(pl.multiple_of(a * 8192 + slab * 1024, 1024), 1024)
+        return pltpu.make_async_copy(grid_ref.at[rows], out_ref.at[rows], sem.at[a, slab])
+
+    def leave(slab):
+        for a in range(2):
+            outward(a, slab).start()
+        return slab + 1
+
+    def after(done, slab):
+        return lax.while_loop(
+            lambda at: (at < 8) & (note_ref[2 + jnp.minimum(at, 7)] <= done), leave, slab
+        )
+
+    held = note_ref[0]
+    slab = add_listed(
+        row_ref, tile_ref, held, SLOTS, data_ref, grid_ref, TX, GROUP_LISTED, after
+    )
+    lax.while_loop(lambda at: at < 8, leave, slab)
+    for slab in range(8):
+        for a in range(2):
+            outward(a, slab).wait()
 
 
 def spread_round(head_ref, data_ref, from_ref, grid_ref, row_ref, tile_ref, sem):
@@ -355,7 +387,7 @@
     copy.start()
     copy.wait()
     held = list_headed(head_ref, row_ref, tile_ref, ROOM, 16)
-    add_listed(row_ref, tile_ref, held, ROOM, data_ref, grid_ref, TX)
+    add_listed(row_ref, tile_ref, held, ROOM, data_ref, grid_ref, TX, GROUP)
 
 
 def quarters(re, im):
@@ -390,7 +422,7 @@
     copy.wait()
     flat = grid_ref.reshape(1024 * DEPTH, CAP)
     sent = sent_ref.reshape(128 * WIDE, CAP)
-    add_listed(row_ref, tile_ref, held, STRAYS, data_ref, flat, DEPTH)
+    add_listed(row_ref, tile_ref, held, STRAYS, data_ref, flat, DEPTH, GROUP)
 
     def columns(n, carry):
         j = 2 * n
@@ -474,8 +506,8 @@
     return pl.BlockSpec(memory_space=pltpu.VMEM)
 
 
-def params():
-    return pltpu.CompilerParams(vmem_limit_bytes=VMEM_LIMIT)
+def params(name):
+    return pltpu.CompilerParams(vmem_limit_bytes=VMEM_MIB.get(name, 40) * MIB)
 
 
 def swap(array, axis):
@@ -488,13 +520,17 @@
         out_shape=out_shape,
         in_specs=in_specs,
         out_specs=out_specs,
-        compiler_params=params(),
+        compiler_params=params(kernel.__name__),
         name=kernel.__name__,
         **options,
     )
 
 
 def anywhere():
+    return pl.BlockSpec(memory_space=pl.ANY)
+
+
+def large():
     return pl.BlockSpec(memory_space=pl.ANY)
 
 
@@ -520,7 +556,7 @@
             spread_and_turn,
             jax.ShapeDtypeStruct((128, 16, 8, CAP), jnp.float32),
             [smem(), smem(), vmem(), vmem(), vmem(), anywhere()],
-            anywhere(),
+            large(),
             scratch_shapes=[
                 pltpu.VMEM((1024, DEPTH, CAP), jnp.float32),
                 pltpu.VMEM((128, WIDE // 8, 8, CAP), jnp.float32),
@@ -561,7 +597,7 @@
     held = held.reshape(128 * 16, CAP)
     strays, rows, tiles, note = call(
         sort_blocks,
-        (rows_of(8 * ROWS_S), ints(392), ints(392), ints(2)),
+        (rows_of(8 * ROWS_S), ints(392), ints(392), ints(16)),
         [smem(), smem(), vmem()],
         (vmem(), smem(), smem(), smem()),
         scratch_shapes=[pltpu.SMEM((392,), jnp.int32), pltpu.SMEM((8,), jnp.int32)],
@@ -571,7 +607,8 @@
         spread_direct,
         rows_of(16384),
         [smem(), smem(), smem(), vmem()],
-        vmem(),
+        large(),
+        scratch_shapes=[pltpu.VMEM((16384, CAP), jnp.float32), pltpu.SemaphoreType.DMA((2, 8))],
         cost_estimate=pl.CostEstimate(flops=3 * 10**10, bytes_accessed=10**8, transcendentals=0),
     )(note, rows, tiles, held)
     stray_heads = strays[:, 5 * STRAYS].astype(jnp.int32)
@@ -625,7 +662,7 @@
         )
         none = jnp.zeros((8, CAP), jnp.int32)
         return finish(
-            jnp.zeros((2,), jnp.int32),
+            jnp.zeros((16,), jnp.int32),
             none,
             jnp.zeros((8 * ROWS_S, CAP), jnp.float32),
             total,

time: 212 us -> 208 us (0.981)
  Pallas kernels: 63.1 us -> 58.5 us
    pallas_call x2, Pallas kernels: 26.8 us -> 22.7 us  [the longest x1 16.1 us: body(): call(spread_direct, rows_of(16384), [smem(), smem(), smem(), vmem()], lar...]
  transfers between devices with their start and end apart: 2 -> 2, of which waited for: 1 -> 1; matrix products, arithmetic and copies ran while one was open for 0% -> 0% of each run, Pallas kernels for 10% -> 8%
where the time goes in v3:
time: 208 us
  waiting for transfers between devices  104 us (50%)
  Pallas kernels  58.5 us (28%)
  blocking collectives  23.5 us (11%)
  starting transfers between devices  18.2 us (9%)
  local copies, waits for them, and re-layouts  2.28 us (1%)
    all_to_all x2, waiting for transfers between devices, swap(): return lax.all_to_all(array, axis, split_axis=0, concat_axis=0, tiled=True)  104 us
    all_to_all x1, blocking collectives, swap(): return lax.all_to_all(array, axis, split_axis=0, concat_axis=0, tiled=True)  23.5 us
    all_to_all x2, starting transfers between devices, swap(): return lax.all_to_all(array, axis, split_axis=0, concat_axis=0, tiled=True)  18.2 us
    pallas_call x1, Pallas kernels, finish(): call(spread_and_turn, jax.ShapeDtypeStruct((128, 16, 8, CAP), jnp.float32...  16.8 us
    pallas_call x1, Pallas kernels, body(): call(spread_direct, rows_of(16384), [smem(), smem(), smem(), vmem()], lar...  16.1 us
    pallas_call x1, Pallas kernels, finish(): call(turn_planes, (jax.ShapeDtypeStruct((2, 4, GRID, GRID), jnp.float32),...  13 us
    pallas_call x1, Pallas kernels, body(): call(sort_blocks, (rows_of(8 * ROWS_S), ints(392), ints(392), ints(16)),...  6.61 us
    pallas_call x1, Pallas kernels, body(): call(pack_blocks, rows_of(128 * 16), [smem()] * 4 + [vmem()] * 2, vmem(),...  6.07 us
  transfers between devices with their start and end apart: 2, of which 1 were waited for; matrix products, arithmetic and copies ran while one was open for 0% of the time, Pallas kernels for 8%

profile of v3, /device:TPU:90, one launch (start us, length us, event | category | flops | bytes accessed | tf_op | source)
XLA Modules:
  0.0 208.3 jit_solution(5840441089171853553)
XLA Ops:
  0.0 6.1 %pack_blocks.1 = f32[2048,128]{1,0:T(8,128)S(1)} custom-call(s32[1]{0:T(128)} %bitcast.5.me_ref, s32[256]{0:T(256)} %bitcast.70, s32[256]{0:T(256)} %bitcast.72, s32[256]{0:T(256)} %bitcast.74, f32[3,256,128]{2,1,0:T(8,128)} %bitcast.62, f32[256,2,128]{2,1,0:T(2,128)} %bitcast.65), custom_call_target="tpu_custom_call" | custom-call | tf_op jit(solution)/shard_map/pack_blocks/pallas_call | solution.py:588
  6.1 23.5 %all_to_all.51 = f32[128,16,128]{2,1,0:T(8,128)S(1)} all-to-all(f32[128,16,128]{2,1,0:T(8,128)S(1)} %bitcast.57), channel_id=1, replica_groups=mesh['brick'=16,'gz'=8] {'brick','gz'}, dimensions={0} | all-to-all | bytes 2097152 | tf_op jit(solution)/shard_map/all_to_all | solution.py:514
  29.6 0.2 fusion
  29.8 0.2 convert_element_type.31.head_ref
  30.0 6.6 %sort_blocks.1 = (f32[1344,128]{1,0:T(8,128)}, s32[392]{0:T(512)S(1)}, s32[392]{0:T(512)S(1)}, s32[16]{0:T(128)S(1)}) custom-call(s32[1]{0:T(128)} %bitcast.5.me_ref, s32[384]{0:T(512)S(1)} %convert_element_type.31.head_ref, f32[2048,128]{1,0:T(8,128)S(1)} %bitcast.55), custom_call_target="tpu_custom_call" | custom-call | tf_op jit(solution)/shard_map/sort_blocks/pallas_call | solution.py:598
  36.7 0.0 copy-start.2
  36.7 0.6 copy-done.2
  37.3 0.6 copy-done.3
  37.8 0.6 copy-done.4
  38.4 4.3 %all-to-all-start.4 = ((f32[8,168,128]{2,1,0:T(8,128)}), f32[8,168,128]{2,1,0:T(8,128)S(1)}, u32[]{:S(2)}, u32[]{:S(2)}) async-start(f32[8,168,128]{2,1,0:T(8,128)} %bitcast.14), calls=%async_computation.4 | async-start | bytes 1376256 | tf_op jit(solution)/shard_map/all_to_all | solution.py:514
  42.8 0.0 copy-done.1
  42.8 16.1 %spread_direct.1 = f32[16384,128]{1,0:T(8,128)} custom-call(s32[16]{0:T(128)} %copy-done.2, s32[392]{0:T(512)} %copy-done.3, s32[392]{0:T(512)} %copy-done.4, f32[2048,128]{1,0:T(8,128)} %bitcast.56), custom_call_target="tpu_custom_call" | custom-call | flops 30000001024 | bytes 100000000 | tf_op jit(solution)/shard_map/spread_direct/pallas_call | solution.py:606
  58.8 0.0 all-to-all-done.4
  58.8 0.0 copy-start.16
  58.9 0.7 convert_bitcast_fusion.head_ref
  59.5 0.3 copy-done.16
  59.8 0.0 copy-done.7
  59.8 0.0 copy-done.9
  59.8 16.8 %spread_and_turn.7 = f32[128,16,8,128]{3,2,1,0:T(8,128)} custom-call(s32[16]{0:T(128)} %copy-done.2, s32[8,128]{1,0:T(8,128)} %convert_bitcast_fusion.head_ref, f32[1344,128]{1,0:T(8,128)} %bitcast.69, bf16[4,256,256]{2,1,0:T(8,128)(2,1)S(1)} %copy-done.7, bf16[4,256,256]{2,1,0:T(8,128)(2,1)S(1)} %copy-done.9, f32[1024,16,128]{2,1,0:T(8,128)} %bitcast.67), custom_call_target="tpu_custom_call" | custom-call | tf_op jit(solution)/shard_map/spread_and_turn/pallas_call | solution.py:555
  76.6 0.0 copy-start.5
  76.6 0.0 copy-start.10
  76.6 13.9 %all-to-all-start.5 = ((f32[128,4,2,16,128]{4,3,2,1,0:T(8,128)}), f32[128,4,2,16,128]{4,3,2,1,0:T(8,128)}, u32[]{:S(2)}, u32[]{:S(2)}) async-start(f32[128,4,2,16,128]{4,3,2,1,0:T(8,128)} %bitcast.61), calls=%async_computation.5 | async-start | bytes 16777216 | tf_op jit(solution)/shard_map/all_to_all | solution.py:514
  90.5 0.0 copy-start.8
  90.5 0.0 copy-start.15
  90.5 0.0 copy-start.17
  90.6 0.0 copy-start.18
  90.6 0.0 copy-start.19
  90.6 103.7 %all-to-all-done.5 = f32[128,4,2,16,128]{4,3,2,1,0:T(8,128)} async-done(((f32[128,4,2,16,128]{4,3,2,1,0:T(8,128)}), f32[128,4,2,16,128]{4,3,2,1,0:T(8,128)}, u32[]{:S(2)}, u32[]{:S(2)}) %all-to-all-start.5) | async-done | bytes 8388640 | tf_op jit(solution)/shard_map/all_to_all | solution.py:514
  194.3 13.0 %turn_planes.7 = (f32[2,4,512,512]{3,2,1,0:T(8,128)}, s32[1]{0:T(128)}) custom-call(f32[4,4,8,4,2,16,128]{6,5,4,3,2,1,0:T(8,128)} %bitcast.19.data_ref, bf16[4,256,256]{2,1,0:T(8,128)(2,1)S(1)} %copy-done.10, bf16[4,256,256]{2,1,0:T(8,128)(2,1)} %constant.101.clone.low_ref, bf16[1024,1024]{1,0:T(8,128)(2,1)S(1)} %copy-done.5), custom_call_target="tpu_custom_call" | custom-call | tf_op jit(solution)/shard_map/turn_planes/pallas_call | solution.py:570
  207.3 0.0 copy-done.8
  207.3 0.0 copy-done.17
  207.3 0.8 while.43
  (13 shorter events, 0.0 us)
Async XLA Ops:
  29.6 13.2 %copy-start.1 = (f32[128,16,128]{2,1,0:T(8,128)}, f32[128,16,128]{2,1,0:T(8,128)S(1)}, u32[]{:S(2)}) copy-start(f32[128,16,128]{2,1,0:T(8,128)S(1)} %all_to_all.51) | copy-start | bytes 3145732
  36.7 0.6 copy-start.2
  37.3 0.6 copy-start.3
  37.8 0.6 copy-start.4
  38.4 20.4 %all-to-all-start.4 = ((f32[8,168,128]{2,1,0:T(8,128)}), f32[8,168,128]{2,1,0:T(8,128)S(1)}, u32[]{:S(2)}, u32[]{:S(2)}) async-start(f32[8,168,128]{2,1,0:T(8,128)} %bitcast.14), calls=%async_computation.4 | async-start | bytes 1376256 | tf_op jit(solution)/shard_map/all_to_all | solution.py:514
  42.8 17.0 %copy-start.7 = (bf16[4,256,256]{2,1,0:T(8,128)(2,1)S(1)}, bf16[4,256,256]{2,1,0:T(8,128)(2,1)}, u32[]{:S(2)}) copy-start(bf16[4,256,256]{2,1,0:T(8,128)(2,1)} %constant.98.clone.high_ref) | copy-start | bytes 1572868
  42.8 17.0 %copy-start.9 = (bf16[4,256,256]{2,1,0:T(8,128)(2,1)S(1)}, bf16[4,256,256]{2,1,0:T(8,128)(2,1)}, u32[]{:S(2)}) copy-start(bf16[4,256,256]{2,1,0:T(8,128)(2,1)} %constant.99.clone.low_ref) | copy-start | bytes 1572868
  58.8 0.9 copy-start.16
  76.6 117.7 %copy-start.5 = (bf16[1024,1024]{1,0:T(8,128)(2,1)S(1)}, bf16[1024,1024]{1,0:T(8,128)(2,1)}, u32[]{:S(2)}) copy-start(bf16[1024,1024]{1,0:T(8,128)(2,1)} %constant.102.clone.y_ref) | copy-start | bytes 6291460
  76.6 117.7 %copy-start.10 = (bf16[4,256,256]{2,1,0:T(8,128)(2,1)S(1)}, bf16[4,256,256]{2,1,0:T(8,128)(2,1)}, u32[]{:S(2)}) copy-start(bf16[4,256,256]{2,1,0:T(8,128)(2,1)} %constant.100.clone.high_ref) | copy-start | bytes 1572868
  76.6 117.7 %all-to-all-start.5 = ((f32[128,4,2,16,128]{4,3,2,1,0:T(8,128)}), f32[128,4,2,16,128]{4,3,2,1,0:T(8,128)}, u32[]{:S(2)}, u32[]{:S(2)}) async-start(f32[128,4,2,16,128]{4,3,2,1,0:T(8,128)} %bitcast.61), calls=%async_computation.5 | async-start | bytes 16777216 | tf_op jit(solution)/shard_map/all_to_all | solution.py:514
  90.5 116.8 %copy-start.8 = (bf16[4,256,256]{2,1,0:T(8,128)(2,1)S(1)}, bf16[4,256,256]{2,1,0:T(8,128)(2,1)}, u32[]{:S(2)}) copy-start(bf16[4,256,256]{2,1,0:T(8,128)(2,1)} %constant.98.clone.high_ref) | copy-start | bytes 1572868
  90.5 116.8 %copy-start.15 = (f32[1,256,2,128]{3,2,1,0:T(2,128)S(1)}, f32[1,256,2,128]{3,2,1,0:T(2,128)}, u32[]{:S(2)}) copy-start(f32[1,256,2,128]{3,2,1,0:T(2,128)} %param.15) | copy-start | bytes 786436
  90.5 116.8 %copy-start.17 = (s32[1,256,1]{1,2,0:T(1,128)S(1)}, s32[1,256,1]{1,2,0:T(1,128)}, u32[]{:S(2)}) copy-start(s32[1,256,1]{1,2,0:T(1,128)} %param.16) | copy-start | bytes 3076
  90.6 116.8 %copy-start.18 = (s32[1,256]{1,0:T(1,128)S(1)}, s32[1,256]{1,0:T(1,128)}, u32[]{:S(2)}) copy-start(s32[1,256]{1,0:T(1,128)} %param.17) | copy-start | bytes 3076
  90.6 116.8 %copy-start.19 = (s32[1,256]{1,0:T(1,128)S(1)}, s32[1,256]{1,0:T(1,128)}, u32[]{:S(2)}) copy-start(s32[1,256]{1,0:T(1,128)} %param.18) | copy-start | bytes 3076
  194.3 13.1 %copy-start.13 = (f32[1,256,3,128]{3,1,2,0:T(8,128)S(1)}, f32[1,256,3,128]{3,1,2,0:T(8,128)}, u32[]{:S(2)}) copy-start(f32[1,256,3,128]{3,1,2,0:T(8,128)} %param.14) | copy-start | bytes 1179652

commit v4 on v3

--- a/solution.py
+++ b/solution.py
@@ -26,6 +26,9 @@
 MARK = 1e30
 GROUP = 16
 GROUP_LISTED = 32
+LISTED = 16
+STRAYED = LISTED + 392
+LIST = STRAYED + 392
 DEPTH = 24
 WIDE = 136
 MIB = 1024 * 1024
@@ -91,7 +94,7 @@
     for b in range(16):
         turn_ref[b] = me_ref[0]
 
-    def direct(i, left):
+    def place(i, left):
         key = brick_ref[i] * 8 + lax.shift_right_logical(tile_ref[i], 4)
         count = count_ref[key]
         place_ref[i] = key * 16 + count
@@ -99,7 +102,7 @@
         left_ref[left] = i
         return left + (count >= SLOTS).astype(jnp.int32)
 
-    strays = lax.fori_loop(0, 256, direct, 0, unroll=4)
+    strays = lax.fori_loop(0, 256, place, 0, unroll=16)
 
     def stray(n, carry):
         i = left_ref[n]
@@ -132,9 +135,7 @@
     lax.fori_loop(0, 256, move, 0, unroll=8)
 
 
-def sort_blocks(
-    me_ref, head_ref, data_ref, out_ref, row_ref, tile_ref, note_ref, left_ref, count_ref
-):
+def sort_blocks(me_ref, head_ref, data_ref, out_ref, list_ref, count_ref):
     lane = lanes()
     me = me_ref[0]
     for t in range(8):
@@ -146,23 +147,20 @@
         source = (n & 15) * 8 + lax.shift_right_logical(n, 4)
         for c in range(SLOTS):
             tile = head_ref[source * SLOTS + c]
-            tx = lax.shift_right_arithmetic(tile, 4)
-            straight = (tx == me).astype(jnp.int32)
-            row_ref[own] = source * 16 + c
-            tile_ref[own] = (source & 7) * 16 + (tile & 15)
-            own = own + straight
-            left_ref[strays] = source * SLOTS + c
-            strays = strays + (tile >= 0).astype(jnp.int32) - straight
-        note_ref[2 + lax.shift_right_logical(n, 4)] = own
+            straight = lax.shift_right_arithmetic(tile, 4) == me
+            at = jnp.where(straight, LISTED + own, STRAYED + strays)
+            list_ref[at] = (source * 16 + c) * 128 + tile
+            own = own + straight.astype(jnp.int32)
+            strays = strays + ((tile >= 0) & ~straight).astype(jnp.int32)
+        list_ref[2 + lax.shift_right_logical(n, 4)] = own
         return own, strays
 
-    own, strays = lax.fori_loop(0, 128, look, (0, 0), unroll=2)
+    own, strays = lax.fori_loop(0, 128, look, (0, 0), unroll=4)
 
     def forward(n, carry):
-        entry = left_ref[n]
-        source = entry // SLOTS
-        row = source * 16 + entry - source * SLOTS
-        tile = head_ref[entry]
+        code = list_ref[STRAYED + n]
+        row = lax.shift_right_logical(code, 7)
+        tile = code & 127
         tx = lax.shift_right_logical(tile, 4)
         k = count_ref[tx]
         count_ref[tx] = k + 1
@@ -172,8 +170,8 @@
                 pl.ds(row + d * SLOTS, 1), :
             ]
         head = pl.ds(tx * ROWS_S + 5 * STRAYS, 1)
-        depth = ((source & 7) * 16 + (tile & 15)).astype(jnp.float32)
-        out_ref[head, :] = jnp.where(lane == k, depth, out_ref[head, :])
+        depth = (row & 112) + (tile & 15)
+        out_ref[head, :] = jnp.where(lane == k, depth.astype(jnp.float32), out_ref[head, :])
         return carry
 
     lax.fori_loop(0, strays, forward, 0)
@@ -184,8 +182,8 @@
         most = jnp.maximum(most, count)
         sent = jnp.minimum(count, STRAYS).astype(jnp.float32)
         out_ref[row : row + 1, :] = jnp.where(lane == LAST, sent, out_ref[row : row + 1, :])
-    note_ref[0] = own
-    note_ref[1] = (most > STRAYS).astype(jnp.int32)
+    list_ref[0] = own
+    list_ref[1] = (most > STRAYS).astype(jnp.int32)
 
 
 def pack_bricks(brick_ref, tile_ref, live_ref, spots_ref, values_ref, out_ref, count_ref):
@@ -314,15 +312,17 @@
     )
 
 
-def add_listed(row_ref, tile_ref, held, step, data_ref, grid_ref, depth, size, after=None):
+def add_listed(find, held, step, data_ref, grid_ref, depth, size, before=None, after=None):
     def group(n, carry):
+        if before is not None:
+            carry = before(jnp.minimum((n + 1) * size, held), carry)
         found = []
         for u in range(size):
             i = n * size + u
             live = i < held
-            i = jnp.where(live, i, 0)
+            row, tile = find(jnp.where(live, i, 0))
             scale = jnp.where(live, 1.0, 0.0).astype(jnp.float32)
-            found.append((tile_ref[i], block_cells(data_ref, row_ref[i], step, scale)))
+            found.append((tile, block_cells(data_ref, row, step, scale)))
         for tile, cells in found:
             for a in range(2):
                 for l in range(TZ):
@@ -335,6 +335,19 @@
     return lax.fori_loop(0, (held + size - 1) // size, group, 0)
 
 
+def direct(list_ref):
+    def find(i):
+        code = list_ref[LISTED + i]
+        row = lax.shift_right_logical(code, 7)
+        return row, (row & 112) + (code & 15)
+
+    return find
+
+
+def listed(row_ref, tile_ref):
+    return lambda i: (row_ref[i], tile_ref[i])
+
+
 def list_headed(head_ref, row_ref, tile_ref, room, base):
     def source(g, total):
         def entry(i, at):
@@ -355,7 +368,36 @@
     lax.fori_loop(0, 16384 // 64, clear, 0, unroll=4)
 
 
-def spread_direct(note_ref, row_ref, tile_ref, data_ref, out_ref, grid_ref, sem):
+def list_strays(head_ref, row_ref, tile_ref, ends_ref, next_ref):
+    for h in range(8):
+        next_ref[h] = 0
+
+    def slab(g, total):
+        def source(h, so_far):
+            held = head_ref[h, LAST]
+
+            def more(state):
+                i, _ = state
+                return (i < held) & (lax.shift_right_logical(head_ref[h, i & 63], 4) == g)
+
+            def entry(state):
+                i, at = state
+                row_ref[at] = h * ROWS_S + i
+                tile_ref[at] = head_ref[h, i]
+                return i + 1, at + 1
+
+            i, so_far = lax.while_loop(more, entry, (next_ref[h], so_far))
+            next_ref[h] = i
+            return so_far
+
+        total = lax.fori_loop(0, 8, source, total)
+        ends_ref[g] = total
+        return total
+
+    return lax.fori_loop(0, 8, slab, 0)
+
+
+def spread_direct(list_ref, data_ref, out_ref, grid_ref, sem):
     clear_grid(grid_ref)
 
     def outward(a, slab):
@@ -369,12 +411,11 @@
 
     def after(done, slab):
         return lax.while_loop(
-            lambda at: (at < 8) & (note_ref[2 + jnp.minimum(at, 7)] <= done), leave, slab
+            lambda at: (at < 8) & (list_ref[2 + jnp.minimum(at, 7)] <= done), leave, slab
         )
 
-    held = note_ref[0]
     slab = add_listed(
-        row_ref, tile_ref, held, SLOTS, data_ref, grid_ref, TX, GROUP_LISTED, after
+        direct(list_ref), list_ref[0], SLOTS, data_ref, grid_ref, TX, GROUP_LISTED, after=after
     )
     lax.while_loop(lambda at: at < 8, leave, slab)
     for slab in range(8):
@@ -387,7 +428,7 @@
     copy.start()
     copy.wait()
     held = list_headed(head_ref, row_ref, tile_ref, ROOM, 16)
-    add_listed(row_ref, tile_ref, held, ROOM, data_ref, grid_ref, TX, GROUP)
+    add_listed(listed(row_ref, tile_ref), held, ROOM, data_ref, grid_ref, TX, GROUP)
 
 
 def quarters(re, im):
@@ -413,16 +454,38 @@
 
 
 def spread_and_turn(
-    note_ref, head_ref, data_ref, high_ref, low_ref, from_ref, out_ref,
-    grid_ref, sent_ref, row_ref, tile_ref, sem, out_sem,
+    list_ref, head_ref, data_ref, high_ref, low_ref, from_ref, out_ref,
+    grid_ref, sent_ref, row_ref, tile_ref, ends_ref, next_ref, sem, out_sem,
 ):
-    copy = pltpu.make_async_copy(from_ref, grid_ref.at[:, pl.ds(0, TX), :], sem)
-    copy.start()
-    held = list_headed(head_ref, row_ref, tile_ref, STRAYS, 0)
-    copy.wait()
+    def inward(a, slab):
+        rows = pl.ds(pl.multiple_of(a * 512 + slab * 64, 64), 64)
+        return pltpu.make_async_copy(
+            from_ref.at[rows], grid_ref.at[rows, pl.ds(0, TX), :], sem.at[a, slab]
+        )
+
+    def arrive(slab):
+        for a in range(2):
+            inward(a, slab).wait()
+        return slab + 1
+
+    for slab in range(8):
+        for a in range(2):
+            inward(a, slab).start()
+    held = list_strays(head_ref, row_ref, tile_ref, ends_ref, next_ref)
     flat = grid_ref.reshape(1024 * DEPTH, CAP)
     sent = sent_ref.reshape(128 * WIDE, CAP)
-    add_listed(row_ref, tile_ref, held, STRAYS, data_ref, flat, DEPTH, GROUP)
+
+    def before(need, slab):
+        return lax.while_loop(
+            lambda at: (at < 8) & ((at == 0) | (ends_ref[jnp.maximum(at - 1, 0)] < need)),
+            arrive,
+            slab,
+        )
+
+    slab = add_listed(
+        listed(row_ref, tile_ref), held, STRAYS, data_ref, flat, DEPTH, GROUP, before=before
+    )
+    lax.while_loop(lambda at: at < 8, arrive, slab)
 
     def columns(n, carry):
         j = 2 * n
@@ -452,7 +515,7 @@
 
     lax.fori_loop(0, 4, columns, 0)
 
-    @pl.when(note_ref[1] > 0)
+    @pl.when(list_ref[1] > 0)
     def _():
         sent[pl.ds(0, 128, stride=WIDE), :] = jnp.full((128, CAP), MARK, jnp.float32)
 
@@ -551,7 +614,7 @@
         values[0],
     )
 
-    def finish(note, heads, data, grid):
+    def finish(blocks, heads, data, grid):
         columns = call(
             spread_and_turn,
             jax.ShapeDtypeStruct((128, 16, 8, CAP), jnp.float32),
@@ -560,12 +623,11 @@
             scratch_shapes=[
                 pltpu.VMEM((1024, DEPTH, CAP), jnp.float32),
                 pltpu.VMEM((128, WIDE // 8, 8, CAP), jnp.float32),
-                pltpu.SMEM((8 * STRAYS,), jnp.int32),
-                pltpu.SMEM((8 * STRAYS,), jnp.int32),
-                pltpu.SemaphoreType.DMA,
+                *[pltpu.SMEM((n,), jnp.int32) for n in (8 * STRAYS, 8 * STRAYS, 8, 8)],
+                pltpu.SemaphoreType.DMA((2, 8)),
                 pltpu.SemaphoreType.DMA((16,)),
             ],
-        )(note, heads, data, z_high, z_low, grid.reshape(1024, TX, CAP))
+        )(blocks, heads, data, z_high, z_low, grid.reshape(1024, TX, CAP))
         planes = swap(columns.reshape(128, 4, 2, TX, CAP), AXES).reshape(4, 4, 8, 4, 2, TX, CAP)
         return call(
             turn_planes,
@@ -595,24 +657,24 @@
     held = swap(sent.reshape(128, 16, CAP), AXES)
     heads = held[:, 15, :SLOTS].astype(jnp.int32).reshape(128 * SLOTS)
     held = held.reshape(128 * 16, CAP)
-    strays, rows, tiles, note = call(
+    strays, blocks = call(
         sort_blocks,
-        (rows_of(8 * ROWS_S), ints(392), ints(392), ints(16)),
+        (rows_of(8 * ROWS_S), ints(LIST)),
         [smem(), smem(), vmem()],
-        (vmem(), smem(), smem(), smem()),
-        scratch_shapes=[pltpu.SMEM((392,), jnp.int32), pltpu.SMEM((8,), jnp.int32)],
+        (vmem(), smem()),
+        scratch_shapes=[pltpu.SMEM((8,), jnp.int32)],
     )(me, heads, held)
     strays = swap(strays.reshape(8, ROWS_S, CAP), "gz")
     grid = call(
         spread_direct,
         rows_of(16384),
-        [smem(), smem(), smem(), vmem()],
+        [smem(), vmem()],
         large(),
         scratch_shapes=[pltpu.VMEM((16384, CAP), jnp.float32), pltpu.SemaphoreType.DMA((2, 8))],
         cost_estimate=pl.CostEstimate(flops=3 * 10**10, bytes_accessed=10**8, transcendentals=0),
-    )(note, rows, tiles, held)
+    )(blocks, held)
     stray_heads = strays[:, 5 * STRAYS].astype(jnp.int32)
-    density, mark = finish(note, stray_heads, strays.reshape(8 * ROWS_S, CAP), grid)
+    density, mark = finish(blocks, stray_heads, strays.reshape(8 * ROWS_S, CAP), grid)
 
     def general(state):
         _, again, *given = lax.optimization_barrier((*state, *points))
@@ -662,7 +724,7 @@
         )
         none = jnp.zeros((8, CAP), jnp.int32)
         return finish(
-            jnp.zeros((16,), jnp.int32),
+            jnp.zeros((LIST,), jnp.int32),
             none,
             jnp.zeros((8 * ROWS_S, CAP), jnp.float32),
             total,

time: 208 us -> 205 us (0.986)
  Pallas kernels: 58.5 us -> 50.7 us
  starting transfers between devices: 18.2 us -> 23.4 us
    all_to_all x2, starting transfers between devices: 18.2 us -> 23.4 us  [swap(): return lax.all_to_all(array, axis, split_axis=0, concat_axis=0, tiled=True)]
    pallas_call x2, Pallas kernels: 22.7 us -> 17.7 us  [the longest x1 13.5 us: body(): call(spread_direct, rows_of(16384), [smem(), vmem()], large(), scratch_sh...]
    pallas_call x1, Pallas kernels: 16.8 us -> 14.5 us  [finish(): call(spread_and_turn, jax.ShapeDtypeStruct((128, 16, 8, CAP), jnp.float32...]
  transfers between devices with their start and end apart: 2 -> 2, of which waited for: 1 -> 1; matrix products, arithmetic and copies ran while one was open for 0% -> 0% of each run, Pallas kernels for 8% -> 7%
where the time goes in v4:
time: 205 us
  waiting for transfers between devices  104 us (51%)
  Pallas kernels  50.7 us (25%)
  blocking collectives  23.8 us (12%)
  starting transfers between devices  23.4 us (11%)
    all_to_all x2, waiting for transfers between devices, swap(): return lax.all_to_all(array, axis, split_axis=0, concat_axis=0, tiled=True)  104 us
    all_to_all x1, blocking collectives, swap(): return lax.all_to_all(array, axis, split_axis=0, concat_axis=0, tiled=True)  23.8 us
    all_to_all x2, starting transfers between devices, swap(): return lax.all_to_all(array, axis, split_axis=0, concat_axis=0, tiled=True)  23.4 us
    pallas_call x1, Pallas kernels, finish(): call(spread_and_turn, jax.ShapeDtypeStruct((128, 16, 8, CAP), jnp.float32...  14.5 us
    pallas_call x1, Pallas kernels, body(): call(spread_direct, rows_of(16384), [smem(), vmem()], large(), scratch_sh...  13.5 us
    pallas_call x1, Pallas kernels, finish(): call(turn_planes, (jax.ShapeDtypeStruct((2, 4, GRID, GRID), jnp.float32),...  13 us
    pallas_call x1, Pallas kernels, body(): call(pack_blocks, rows_of(128 * 16), [smem()] * 4 + [vmem()] * 2, vmem(),...  5.56 us
    pallas_call x1, Pallas kernels, body(): call(sort_blocks, (rows_of(8 * ROWS_S), ints(LIST)), [smem(), smem(), vme...  4.2 us
  transfers between devices with their start and end apart: 2, of which 1 were waited for; matrix products, arithmetic and copies ran while one was open for 0% of the time, Pallas kernels for 7%

profile of v4, /device:TPU:90, one launch (start us, length us, event | category | flops | bytes accessed | tf_op | source)
XLA Modules:
  0.0 204.9 jit_solution(8252111031937747046)
XLA Ops:
  0.0 5.6 %pack_blocks.1 = f32[2048,128]{1,0:T(8,128)S(1)} custom-call(s32[1]{0:T(128)} %bitcast.5.me_ref, s32[256]{0:T(256)} %bitcast.70, s32[256]{0:T(256)} %bitcast.72, s32[256]{0:T(256)} %bitcast.74, f32[3,256,128]{2,1,0:T(8,128)} %bitcast.62, f32[256,2,128]{2,1,0:T(2,128)} %bitcast.65), custom_call_target="tpu_custom_call" | custom-call | tf_op jit(solution)/shard_map/pack_blocks/pallas_call | solution.py:650
  5.6 23.8 %all_to_all.51 = f32[128,16,128]{2,1,0:T(8,128)S(1)} all-to-all(f32[128,16,128]{2,1,0:T(8,128)S(1)} %bitcast.57), channel_id=1, replica_groups=mesh['brick'=16,'gz'=8] {'brick','gz'}, dimensions={0} | all-to-all | bytes 2097152 | tf_op jit(solution)/shard_map/all_to_all | solution.py:577
  29.3 0.2 fusion
  29.6 0.2 convert_element_type.31.head_ref
  29.8 4.2 %sort_blocks.1 = (f32[1344,128]{1,0:T(8,128)}, s32[800]{0:T(1024)S(1)}) custom-call(s32[1]{0:T(128)} %bitcast.5.me_ref, s32[384]{0:T(512)S(1)} %convert_element_type.31.head_ref, f32[2048,128]{1,0:T(8,128)S(1)} %bitcast.55), custom_call_target="tpu_custom_call" | custom-call | tf_op jit(solution)/shard_map/sort_blocks/pallas_call | solution.py:660
  34.0 0.0 copy-start.2
  34.0 0.6 copy-done.2
  34.6 4.9 %all-to-all-start.4 = ((f32[8,168,128]{2,1,0:T(8,128)}), f32[8,168,128]{2,1,0:T(8,128)S(1)}, u32[]{:S(2)}, u32[]{:S(2)}) async-start(f32[8,168,128]{2,1,0:T(8,128)} %bitcast.14), calls=%async_computation.4 | async-start | bytes 1376256 | tf_op jit(solution)/shard_map/all_to_all | solution.py:577
  39.5 0.0 copy-done.1
  39.5 13.5 %spread_direct.1 = f32[16384,128]{1,0:T(8,128)} custom-call(s32[800]{0:T(1024)} %copy-done.2, f32[2048,128]{1,0:T(8,128)} %bitcast.56), custom_call_target="tpu_custom_call" | custom-call | flops 30000001024 | bytes 100000000 | tf_op jit(solution)/shard_map/spread_direct/pallas_call | solution.py:668
  53.0 0.0 all-to-all-done.4
  53.0 0.0 copy-start.14
  53.0 0.7 convert_bitcast_fusion.head_ref
  53.7 0.2 copy-done.14
  53.9 0.0 copy-done.5
  53.9 0.0 copy-done.7
  53.9 14.5 %spread_and_turn.7 = f32[128,16,8,128]{3,2,1,0:T(8,128)} custom-call(s32[800]{0:T(1024)} %copy-done.2, s32[8,128]{1,0:T(8,128)} %convert_bitcast_fusion.head_ref, f32[1344,128]{1,0:T(8,128)} %bitcast.69, bf16[4,256,256]{2,1,0:T(8,128)(2,1)S(1)} %copy-done.5, bf16[4,256,256]{2,1,0:T(8,128)(2,1)S(1)} %copy-done.7, f32[1024,16,128]{2,1,0:T(8,128)} %bitcast.67), custom_call_target="tpu_custom_call" | custom-call | tf_op jit(solution)/shard_map/spread_and_turn/pallas_call | solution.py:618
  68.4 0.0 copy-start.3
  68.4 0.0 copy-start.8
  68.5 18.5 %all-to-all-start.5 = ((f32[128,4,2,16,128]{4,3,2,1,0:T(8,128)}), f32[128,4,2,16,128]{4,3,2,1,0:T(8,128)}, u32[]{:S(2)}, u32[]{:S(2)}) async-start(f32[128,4,2,16,128]{4,3,2,1,0:T(8,128)} %bitcast.61), calls=%async_computation.5 | async-start | bytes 16777216 | tf_op jit(solution)/shard_map/all_to_all | solution.py:577
  87.0 0.0 copy-start.6
  87.0 0.0 copy-start.13
  87.0 0.0 copy-start.15
  87.0 0.0 copy-start.16
  87.1 0.0 copy-start.17
  87.1 103.7 %all-to-all-done.5 = f32[128,4,2,16,128]{4,3,2,1,0:T(8,128)} async-done(((f32[128,4,2,16,128]{4,3,2,1,0:T(8,128)}), f32[128,4,2,16,128]{4,3,2,1,0:T(8,128)}, u32[]{:S(2)}, u32[]{:S(2)}) %all-to-all-start.5) | async-done | bytes 8388640 | tf_op jit(solution)/shard_map/all_to_all | solution.py:577
  190.8 0.0 copy-done.3
  190.8 0.0 copy-done.8
  190.8 13.0 %turn_planes.7 = (f32[2,4,512,512]{3,2,1,0:T(8,128)}, s32[1]{0:T(128)}) custom-call(f32[4,4,8,4,2,16,128]{6,5,4,3,2,1,0:T(8,128)} %bitcast.19.data_ref, bf16[4,256,256]{2,1,0:T(8,128)(2,1)S(1)} %copy-done.8, bf16[4,256,256]{2,1,0:T(8,128)(2,1)} %constant.101.clone.low_ref, bf16[1024,1024]{1,0:T(8,128)(2,1)S(1)} %copy-done.3), custom_call_target="tpu_custom_call" | custom-call | tf_op jit(solution)/shard_map/turn_planes/pallas_call | solution.py:632
  203.8 0.0 copy-done.6
  203.8 0.0 copy-done.13
  203.8 0.9 while.43
  (9 shorter events, 0.0 us)
Async XLA Ops:
  29.3 10.1 %copy-start.1 = (f32[128,16,128]{2,1,0:T(8,128)}, f32[128,16,128]{2,1,0:T(8,128)S(1)}, u32[]{:S(2)}) copy-start(f32[128,16,128]{2,1,0:T(8,128)S(1)} %all_to_all.51) | copy-start | bytes 3145732
  34.0 0.6 copy-start.2
  34.6 18.4 %all-to-all-start.4 = ((f32[8,168,128]{2,1,0:T(8,128)}), f32[8,168,128]{2,1,0:T(8,128)S(1)}, u32[]{:S(2)}, u32[]{:S(2)}) async-start(f32[8,168,128]{2,1,0:T(8,128)} %bitcast.14), calls=%async_computation.4 | async-start | bytes 1376256 | tf_op jit(solution)/shard_map/all_to_all | solution.py:577
  39.5 14.5 %copy-start.5 = (bf16[4,256,256]{2,1,0:T(8,128)(2,1)S(1)}, bf16[4,256,256]{2,1,0:T(8,128)(2,1)}, u32[]{:S(2)}) copy-start(bf16[4,256,256]{2,1,0:T(8,128)(2,1)} %constant.98.clone.high_ref) | copy-start | bytes 1572868
  39.5 14.5 %copy-start.7 = (bf16[4,256,256]{2,1,0:T(8,128)(2,1)S(1)}, bf16[4,256,256]{2,1,0:T(8,128)(2,1)}, u32[]{:S(2)}) copy-start(bf16[4,256,256]{2,1,0:T(8,128)(2,1)} %constant.99.clone.low_ref) | copy-start | bytes 1572868
  53.0 0.9 copy-start.14
  68.4 122.4 %copy-start.3 = (bf16[1024,1024]{1,0:T(8,128)(2,1)S(1)}, bf16[1024,1024]{1,0:T(8,128)(2,1)}, u32[]{:S(2)}) copy-start(bf16[1024,1024]{1,0:T(8,128)(2,1)} %constant.102.clone.y_ref) | copy-start | bytes 6291460
  68.4 122.3 %copy-start.8 = (bf16[4,256,256]{2,1,0:T(8,128)(2,1)S(1)}, bf16[4,256,256]{2,1,0:T(8,128)(2,1)}, u32[]{:S(2)}) copy-start(bf16[4,256,256]{2,1,0:T(8,128)(2,1)} %constant.100.clone.high_ref) | copy-start | bytes 1572868
  68.5 122.3 %all-to-all-start.5 = ((f32[128,4,2,16,128]{4,3,2,1,0:T(8,128)}), f32[128,4,2,16,128]{4,3,2,1,0:T(8,128)}, u32[]{:S(2)}, u32[]{:S(2)}) async-start(f32[128,4,2,16,128]{4,3,2,1,0:T(8,128)} %bitcast.61), calls=%async_computation.5 | async-start | bytes 16777216 | tf_op jit(solution)/shard_map/all_to_all | solution.py:577
  87.0 116.8 %copy-start.6 = (bf16[4,256,256]{2,1,0:T(8,128)(2,1)S(1)}, bf16[4,256,256]{2,1,0:T(8,128)(2,1)}, u32[]{:S(2)}) copy-start(bf16[4,256,256]{2,1,0:T(8,128)(2,1)} %constant.98.clone.high_ref) | copy-start | bytes 1572868
  87.0 116.8 %copy-start.13 = (f32[1,256,2,128]{3,2,1,0:T(2,128)S(1)}, f32[1,256,2,128]{3,2,1,0:T(2,128)}, u32[]{:S(2)}) copy-start(f32[1,256,2,128]{3,2,1,0:T(2,128)} %param.15) | copy-start | bytes 786436
  87.0 116.8 %copy-start.15 = (s32[1,256,1]{1,2,0:T(1,128)S(1)}, s32[1,256,1]{1,2,0:T(1,128)}, u32[]{:S(2)}) copy-start(s32[1,256,1]{1,2,0:T(1,128)} %param.16) | copy-start | bytes 3076
  87.0 116.8 %copy-start.16 = (s32[1,256]{1,0:T(1,128)S(1)}, s32[1,256]{1,0:T(1,128)}, u32[]{:S(2)}) copy-start(s32[1,256]{1,0:T(1,128)} %param.17) | copy-start | bytes 3076
  87.1 116.8 %copy-start.17 = (s32[1,256]{1,0:T(1,128)S(1)}, s32[1,256]{1,0:T(1,128)}, u32[]{:S(2)}) copy-start(s32[1,256]{1,0:T(1,128)} %param.18) | copy-start | bytes 3076
  190.8 13.0 %copy-start.11 = (f32[1,256,3,128]{3,1,2,0:T(8,128)S(1)}, f32[1,256,3,128]{3,1,2,0:T(8,128)}, u32[]{:S(2)}) copy-start(f32[1,256,3,128]{3,1,2,0:T(8,128)} %param.14) | copy-start | bytes 1179652

commit v5 on v4

--- a/solution.py
+++ b/solution.py
@@ -24,8 +24,7 @@
 STRAYS = 32
 ROWS_S = 5 * STRAYS + 8
 MARK = 1e30
-GROUP = 16
-GROUP_LISTED = 32
+GROUP = 32
 LISTED = 16
 STRAYED = LISTED + 392
 LIST = STRAYED + 392
@@ -415,7 +414,7 @@
         )
 
     slab = add_listed(
-        direct(list_ref), list_ref[0], SLOTS, data_ref, grid_ref, TX, GROUP_LISTED, after=after
+        direct(list_ref), list_ref[0], SLOTS, data_ref, grid_ref, TX, GROUP, after=after
     )
     lax.while_loop(lambda at: at < 8, leave, slab)
     for slab in range(8):
@@ -450,7 +449,7 @@
     def dot(a, b):
         return jnp.dot(a, b, preferred_element_type=jnp.float32)
 
-    return dot(high, top) + (dot(high, rest) + dot(low, top))
+    return (dot(high, top) + dot(high, rest)) + dot(low, top)
 
 
 def spread_and_turn(
@@ -513,7 +512,7 @@
     def outward(n):
         return pltpu.make_async_copy(sent_ref.at[:, n], out_ref.at[:, n], out_sem.at[n])
 
-    lax.fori_loop(0, 4, columns, 0)
+    lax.fori_loop(0, 4, columns, 0, unroll=2)
 
     @pl.when(list_ref[1] > 0)
     def _():
@@ -521,7 +520,7 @@
 
     for n in range(8):
         outward(2 * n).start()
-    lax.fori_loop(4, 8, columns, 0)
+    lax.fori_loop(4, 8, columns, 0, unroll=2)
     for n in range(8):
         outward(2 * n + 1).start()
     for n in range(16):

time: 205 us -> 203 us (level)
  Pallas kernels: 50.7 us -> 45.9 us
    pallas_call x1, Pallas kernels: 13.5 us -> 10.3 us  [body(): call(spread_direct, rows_of(16384), [smem(), vmem()], large(), scratch_sh...]
  transfers between devices with their start and end apart: 2 -> 2, of which waited for: 1 -> 2; matrix products, arithmetic and copies ran while one was open for 0% -> 0% of each run, Pallas kernels for 7% -> 5%
where the time goes in v5:
time: 203 us; the launch traced here: 202 us
  waiting for transfers between devices  104 us (51%)
  Pallas kernels  45.9 us (23%)
  starting transfers between devices  24.8 us (12%)
  blocking collectives  24.2 us (12%)
    all_to_all x2, waiting for transfers between devices, swap(): return lax.all_to_all(array, axis, split_axis=0, concat_axis=0, tiled=True)  104 us
    all_to_all x2, starting transfers between devices, swap(): return lax.all_to_all(array, axis, split_axis=0, concat_axis=0, tiled=True)  24.8 us
    all_to_all x1, blocking collectives, swap(): return lax.all_to_all(array, axis, split_axis=0, concat_axis=0, tiled=True)  24.2 us
    pallas_call x1, Pallas kernels, finish(): call(spread_and_turn, jax.ShapeDtypeStruct((128, 16, 8, CAP), jnp.float32...  13.8 us
    pallas_call x1, Pallas kernels, finish(): call(turn_planes, (jax.ShapeDtypeStruct((2, 4, GRID, GRID), jnp.float32),...  12.6 us
    pallas_call x1, Pallas kernels, body(): call(spread_direct, rows_of(16384), [smem(), vmem()], large(), scratch_sh...  10.3 us
    pallas_call x1, Pallas kernels, body(): call(pack_blocks, rows_of(128 * 16), [smem()] * 4 + [vmem()] * 2, vmem(),...  5.17 us
  transfers between devices with their start and end apart: 2, of which 2 were waited for; matrix products, arithmetic and copies ran while one was open for 0% of the time, Pallas kernels for 5%

profile of v5, /device:TPU:90, one launch (start us, length us, event | category | flops | bytes accessed | tf_op | source)
XLA Modules:
  0.0 202.1 jit_solution(1201384375749604035)
XLA Ops:
  0.0 5.2 %pack_blocks.1 = f32[2048,128]{1,0:T(8,128)S(1)} custom-call(s32[1]{0:T(128)} %bitcast.5.me_ref, s32[256]{0:T(256)} %bitcast.70, s32[256]{0:T(256)} %bitcast.72, s32[256]{0:T(256)} %bitcast.74, f32[3,256,128]{2,1,0:T(8,128)} %bitcast.62, f32[256,2,128]{2,1,0:T(2,128)} %bitcast.65), custom_call_target="tpu_custom_call" | custom-call | tf_op jit(solution)/shard_map/pack_blocks/pallas_call | solution.py:649
  5.2 24.2 %all_to_all.51 = f32[128,16,128]{2,1,0:T(8,128)S(1)} all-to-all(f32[128,16,128]{2,1,0:T(8,128)S(1)} %bitcast.57), channel_id=1, replica_groups=mesh['brick'=16,'gz'=8] {'brick','gz'}, dimensions={0} | all-to-all | bytes 2097152 | tf_op jit(solution)/shard_map/all_to_all | solution.py:576
  29.4 0.2 fusion
  29.6 0.2 convert_element_type.31.head_ref
  29.8 4.0 %sort_blocks.1 = (f32[1344,128]{1,0:T(8,128)}, s32[800]{0:T(1024)S(1)}) custom-call(s32[1]{0:T(128)} %bitcast.5.me_ref, s32[384]{0:T(512)S(1)} %convert_element_type.31.head_ref, f32[2048,128]{1,0:T(8,128)S(1)} %bitcast.55), custom_call_target="tpu_custom_call" | custom-call | tf_op jit(solution)/shard_map/sort_blocks/pallas_call | solution.py:659
  33.8 0.0 copy-start.2
  33.8 0.6 copy-done.2
  34.4 4.8 %all-to-all-start.4 = ((f32[8,168,128]{2,1,0:T(8,128)}), f32[8,168,128]{2,1,0:T(8,128)S(1)}, u32[]{:S(2)}, u32[]{:S(2)}) async-start(f32[8,168,128]{2,1,0:T(8,128)} %bitcast.14), calls=%async_computation.4 | async-start | bytes 1376256 | tf_op jit(solution)/shard_map/all_to_all | solution.py:576
  39.2 0.0 copy-done.1
  39.2 10.3 %spread_direct.1 = f32[16384,128]{1,0:T(8,128)} custom-call(s32[800]{0:T(1024)} %copy-done.2, f32[2048,128]{1,0:T(8,128)} %bitcast.56), custom_call_target="tpu_custom_call" | custom-call | flops 30000001024 | bytes 100000000 | tf_op jit(solution)/shard_map/spread_direct/pallas_call | solution.py:667
  49.5 0.3 all-to-all-done.4
  49.9 0.7 convert_bitcast_fusion.head_ref
  50.6 0.3 copy-done.14
  50.8 0.0 copy-done.5
  50.8 0.0 copy-done.7
  50.8 13.8 %spread_and_turn.7 = f32[128,16,8,128]{3,2,1,0:T(8,128)} custom-call(s32[800]{0:T(1024)} %copy-done.2, s32[8,128]{1,0:T(8,128)} %convert_bitcast_fusion.head_ref, f32[1344,128]{1,0:T(8,128)} %bitcast.69, bf16[4,256,256]{2,1,0:T(8,128)(2,1)S(1)} %copy-done.5, bf16[4,256,256]{2,1,0:T(8,128)(2,1)S(1)} %copy-done.7, f32[1024,16,128]{2,1,0:T(8,128)} %bitcast.67), custom_call_target="tpu_custom_call" | custom-call | tf_op jit(solution)/shard_map/spread_and_turn/pallas_call | solution.py:617
  64.6 0.0 copy-start.3
  64.7 0.0 copy-start.8
  64.7 20.0 %all-to-all-start.5 = ((f32[128,4,2,16,128]{4,3,2,1,0:T(8,128)}), f32[128,4,2,16,128]{4,3,2,1,0:T(8,128)}, u32[]{:S(2)}, u32[]{:S(2)}) async-start(f32[128,4,2,16,128]{4,3,2,1,0:T(8,128)} %bitcast.61), calls=%async_computation.5 | async-start | bytes 16777216 | tf_op jit(solution)/shard_map/all_to_all | solution.py:576
  84.7 0.0 copy-start.6
  84.7 0.0 copy-start.13
  84.7 0.0 copy-start.15
  84.7 0.0 copy-start.16
  84.8 0.0 copy-start.17
  84.8 103.7 %all-to-all-done.5 = f32[128,4,2,16,128]{4,3,2,1,0:T(8,128)} async-done(((f32[128,4,2,16,128]{4,3,2,1,0:T(8,128)}), f32[128,4,2,16,128]{4,3,2,1,0:T(8,128)}, u32[]{:S(2)}, u32[]{:S(2)}) %all-to-all-start.5) | async-done | bytes 8388640 | tf_op jit(solution)/shard_map/all_to_all | solution.py:576
  188.5 0.0 copy-done.3
  188.5 0.0 copy-done.8
  188.5 12.6 %turn_planes.7 = (f32[2,4,512,512]{3,2,1,0:T(8,128)}, s32[1]{0:T(128)}) custom-call(f32[4,4,8,4,2,16,128]{6,5,4,3,2,1,0:T(8,128)} %bitcast.19.data_ref, bf16[4,256,256]{2,1,0:T(8,128)(2,1)S(1)} %copy-done.8, bf16[4,256,256]{2,1,0:T(8,128)(2,1)} %constant.101.clone.low_ref, bf16[1024,1024]{1,0:T(8,128)(2,1)S(1)} %copy-done.3), custom_call_target="tpu_custom_call" | custom-call | tf_op jit(solution)/shard_map/turn_planes/pallas_call | solution.py:631
  201.1 0.0 copy-done.6
  201.1 0.0 copy-done.13
  201.1 0.0 copy-done.15
  201.1 0.9 while.43
  (9 shorter events, 0.0 us)
Async XLA Ops:
  29.4 9.9 %copy-start.1 = (f32[128,16,128]{2,1,0:T(8,128)}, f32[128,16,128]{2,1,0:T(8,128)S(1)}, u32[]{:S(2)}) copy-start(f32[128,16,128]{2,1,0:T(8,128)S(1)} %all_to_all.51) | copy-start | bytes 3145732
  33.8 0.6 copy-start.2
  34.4 15.5 %all-to-all-start.4 = ((f32[8,168,128]{2,1,0:T(8,128)}), f32[8,168,128]{2,1,0:T(8,128)S(1)}, u32[]{:S(2)}, u32[]{:S(2)}) async-start(f32[8,168,128]{2,1,0:T(8,128)} %bitcast.14), calls=%async_computation.4 | async-start | bytes 1376256 | tf_op jit(solution)/shard_map/all_to_all | solution.py:576
  39.2 11.6 %copy-start.5 = (bf16[4,256,256]{2,1,0:T(8,128)(2,1)S(1)}, bf16[4,256,256]{2,1,0:T(8,128)(2,1)}, u32[]{:S(2)}) copy-start(bf16[4,256,256]{2,1,0:T(8,128)(2,1)} %constant.98.clone.high_ref) | copy-start | bytes 1572868
  39.2 11.6 %copy-start.7 = (bf16[4,256,256]{2,1,0:T(8,128)(2,1)S(1)}, bf16[4,256,256]{2,1,0:T(8,128)(2,1)}, u32[]{:S(2)}) copy-start(bf16[4,256,256]{2,1,0:T(8,128)(2,1)} %constant.99.clone.low_ref) | copy-start | bytes 1572868
  49.9 0.9 copy-start.14
  64.6 123.8 %copy-start.3 = (bf16[1024,1024]{1,0:T(8,128)(2,1)S(1)}, bf16[1024,1024]{1,0:T(8,128)(2,1)}, u32[]{:S(2)}) copy-start(bf16[1024,1024]{1,0:T(8,128)(2,1)} %constant.102.clone.y_ref) | copy-start | bytes 6291460
  64.7 123.8 %copy-start.8 = (bf16[4,256,256]{2,1,0:T(8,128)(2,1)S(1)}, bf16[4,256,256]{2,1,0:T(8,128)(2,1)}, u32[]{:S(2)}) copy-start(bf16[4,256,256]{2,1,0:T(8,128)(2,1)} %constant.100.clone.high_ref) | copy-start | bytes 1572868
  64.7 123.8 %all-to-all-start.5 = ((f32[128,4,2,16,128]{4,3,2,1,0:T(8,128)}), f32[128,4,2,16,128]{4,3,2,1,0:T(8,128)}, u32[]{:S(2)}, u32[]{:S(2)}) async-start(f32[128,4,2,16,128]{4,3,2,1,0:T(8,128)} %bitcast.61), calls=%async_computation.5 | async-start | bytes 16777216 | tf_op jit(solution)/shard_map/all_to_all | solution.py:576
  84.7 116.4 %copy-start.6 = (bf16[4,256,256]{2,1,0:T(8,128)(2,1)S(1)}, bf16[4,256,256]{2,1,0:T(8,128)(2,1)}, u32[]{:S(2)}) copy-start(bf16[4,256,256]{2,1,0:T(8,128)(2,1)} %constant.98.clone.high_ref) | copy-start | bytes 1572868
  84.7 116.3 %copy-start.13 = (f32[1,256,2,128]{3,2,1,0:T(2,128)S(1)}, f32[1,256,2,128]{3,2,1,0:T(2,128)}, u32[]{:S(2)}) copy-start(f32[1,256,2,128]{3,2,1,0:T(2,128)} %param.15) | copy-start | bytes 786436
  84.7 116.3 %copy-start.15 = (s32[1,256,1]{1,2,0:T(1,128)S(1)}, s32[1,256,1]{1,2,0:T(1,128)}, u32[]{:S(2)}) copy-start(s32[1,256,1]{1,2,0:T(1,128)} %param.16) | copy-start | bytes 3076
  84.7 116.3 %copy-start.16 = (s32[1,256]{1,0:T(1,128)S(1)}, s32[1,256]{1,0:T(1,128)}, u32[]{:S(2)}) copy-start(s32[1,256]{1,0:T(1,128)} %param.17) | copy-start | bytes 3076
  84.8 116.3 %copy-start.17 = (s32[1,256]{1,0:T(1,128)S(1)}, s32[1,256]{1,0:T(1,128)}, u32[]{:S(2)}) copy-start(s32[1,256]{1,0:T(1,128)} %param.18) | copy-start | bytes 3076
  188.5 12.6 %copy-start.11 = (f32[1,256,3,128]{3,1,2,0:T(8,128)S(1)}, f32[1,256,3,128]{3,1,2,0:T(8,128)}, u32[]{:S(2)}) copy-start(f32[1,256,3,128]{3,1,2,0:T(8,128)} %param.14) | copy-start | bytes 1179652

commit v6 on v5

--- a/solution.py
+++ b/solution.py
@@ -154,7 +154,7 @@
         list_ref[2 + lax.shift_right_logical(n, 4)] = own
         return own, strays
 
-    own, strays = lax.fori_loop(0, 128, look, (0, 0), unroll=4)
+    own, strays = lax.fori_loop(0, 128, look, (0, 0), unroll=8)
 
     def forward(n, carry):
         code = list_ref[STRAYED + n]
@@ -512,7 +512,7 @@
     def outward(n):
         return pltpu.make_async_copy(sent_ref.at[:, n], out_ref.at[:, n], out_sem.at[n])
 
-    lax.fori_loop(0, 4, columns, 0, unroll=2)
+    lax.fori_loop(0, 4, columns, 0, unroll=4)
 
     @pl.when(list_ref[1] > 0)
     def _():
@@ -520,14 +520,14 @@
 
     for n in range(8):
         outward(2 * n).start()
-    lax.fori_loop(4, 8, columns, 0, unroll=2)
+    lax.fori_loop(4, 8, columns, 0, unroll=4)
     for n in range(8):
         outward(2 * n + 1).start()
     for n in range(16):
         outward(n).wait()
 
 
-def turn_planes(data_ref, high_ref, low_ref, y_ref, out_ref, mark_ref, rows_ref, left_ref):
+def turn_planes(data_ref, high_ref, low_ref, y_ref, out_ref, mark_ref, rows_ref):
     @pl.when(pl.program_id(0) == 0)
     def _():
         most = data_ref[0, 0, :, 0, 0, 0]
@@ -550,13 +550,12 @@
                     rows_ref[pl.ds(start, 128, stride=4), :] = turned[
                         a * 128 : (a + 1) * 128, u * 128 : (u + 1) * 128
                     ]
-    for n in range(8):
-        left_ref[:, n * 128 : (n + 1) * 128] = rows_ref[n * GRID : (n + 1) * GRID, :].astype(
-            jnp.bfloat16
-        )
+    left = jnp.concatenate(
+        [rows_ref[n * GRID : (n + 1) * GRID, :].astype(jnp.bfloat16) for n in range(8)], axis=1
+    )
     for n in range(4):
         out_ref[n // 2, 0, :, (n % 2) * 256 : (n % 2 + 1) * 256] = jnp.dot(
-            left_ref[...], y_ref[:, n * 256 : (n + 1) * 256], preferred_element_type=jnp.float32
+            left, y_ref[:, n * 256 : (n + 1) * 256], preferred_element_type=jnp.float32
         )
 
 
@@ -639,10 +638,7 @@
             ],
             (pl.BlockSpec((2, 1, GRID, GRID), lambda q: (0, q, 0, 0)), smem()),
             grid=(4,),
-            scratch_shapes=[
-                pltpu.VMEM((8 * GRID, CAP), jnp.float32),
-                pltpu.VMEM((GRID, 2 * GRID), jnp.bfloat16),
-            ],
+            scratch_shapes=[pltpu.VMEM((8 * GRID, CAP), jnp.float32)],
         )(planes, x_high, x_low, y_table)
 
     me = lax.axis_index("gz").astype(jnp.int32).reshape(1)

time: 203 us -> 202 us (level)
  Pallas kernels: 45.9 us -> 51 us
  starting transfers between devices: 24.8 us -> 20.9 us
    pallas_call x1, Pallas kernels: 10.3 us -> 14.9 us  [body(): call(spread_direct, rows_of(16384), [smem(), vmem()], large(), scratch_sh...]
    all_to_all x2, starting transfers between devices: 24.8 us -> 20.9 us  [swap(): return lax.all_to_all(array, axis, split_axis=0, concat_axis=0, tiled=True)]
  transfers between devices with their start and end apart: 2 -> 2, of which waited for: 2 -> 1; matrix products, arithmetic and copies ran while one was open for 0% -> 0% of each run, Pallas kernels for 5% -> 7%
where the time goes in v6:
time: 202 us; the launch traced here: 203 us
  waiting for transfers between devices  104 us (51%)
  Pallas kernels  51 us (25%)
  blocking collectives  23.9 us (12%)
  starting transfers between devices  20.9 us (10%)
    all_to_all x2, waiting for transfers between devices, swap(): return lax.all_to_all(array, axis, split_axis=0, concat_axis=0, tiled=True)  104 us
    all_to_all x1, blocking collectives, swap(): return lax.all_to_all(array, axis, split_axis=0, concat_axis=0, tiled=True)  23.9 us
    all_to_all x2, starting transfers between devices, swap(): return lax.all_to_all(array, axis, split_axis=0, concat_axis=0, tiled=True)  20.9 us
    pallas_call x1, Pallas kernels, body(): call(spread_direct, rows_of(16384), [smem(), vmem()], large(), scratch_sh...  14.9 us
    pallas_call x1, Pallas kernels, finish(): call(spread_and_turn, jax.ShapeDtypeStruct((128, 16, 8, CAP), jnp.float32...  13.7 us
    pallas_call x1, Pallas kernels, finish(): call(turn_planes, (jax.ShapeDtypeStruct((2, 4, GRID, GRID), jnp.float32),...  12.3 us
    pallas_call x1, Pallas kernels, body(): call(pack_blocks, rows_of(128 * 16), [smem()] * 4 + [vmem()] * 2, vmem(),...  5.59 us
    pallas_call x1, Pallas kernels, body(): call(sort_blocks, (rows_of(8 * ROWS_S), ints(LIST)), [smem(), smem(), vme...  4.48 us
  transfers between devices with their start and end apart: 2, of which 1 were waited for; matrix products, arithmetic and copies ran while one was open for 0% of the time, Pallas kernels for 7%

profile of v6, /device:TPU:90, one launch (start us, length us, event | category | flops | bytes accessed | tf_op | source)
XLA Modules:
  0.0 202.6 jit_solution(14912060244497629349)
XLA Ops:
  0.0 5.6 %pack_blocks.1 = f32[2048,128]{1,0:T(8,128)S(1)} custom-call(s32[1]{0:T(128)} %bitcast.5.me_ref, s32[256]{0:T(256)} %bitcast.70, s32[256]{0:T(256)} %bitcast.72, s32[256]{0:T(256)} %bitcast.74, f32[3,256,128]{2,1,0:T(8,128)} %bitcast.62, f32[256,2,128]{2,1,0:T(2,128)} %bitcast.65), custom_call_target="tpu_custom_call" | custom-call | tf_op jit(solution)/shard_map/pack_blocks/pallas_call | solution.py:645
  5.6 23.9 %all_to_all.51 = f32[128,16,128]{2,1,0:T(8,128)S(1)} all-to-all(f32[128,16,128]{2,1,0:T(8,128)S(1)} %bitcast.57), channel_id=1, replica_groups=mesh['brick'=16,'gz'=8] {'brick','gz'}, dimensions={0} | all-to-all | bytes 2097152 | tf_op jit(solution)/shard_map/all_to_all | solution.py:575
  29.5 0.2 fusion
  29.7 0.2 convert_element_type.31.head_ref
  29.9 4.5 %sort_blocks.1 = (f32[1344,128]{1,0:T(8,128)}, s32[800]{0:T(1024)S(1)}) custom-call(s32[1]{0:T(128)} %bitcast.5.me_ref, s32[384]{0:T(512)S(1)} %convert_element_type.31.head_ref, f32[2048,128]{1,0:T(8,128)S(1)} %bitcast.55), custom_call_target="tpu_custom_call" | custom-call | tf_op jit(solution)/shard_map/sort_blocks/pallas_call | solution.py:655
  34.4 0.0 copy-start.2
  34.4 0.6 copy-done.2
  35.0 4.8 %all-to-all-start.4 = ((f32[8,168,128]{2,1,0:T(8,128)}), f32[8,168,128]{2,1,0:T(8,128)S(1)}, u32[]{:S(2)}, u32[]{:S(2)}) async-start(f32[8,168,128]{2,1,0:T(8,128)} %bitcast.14), calls=%async_computation.4 | async-start | bytes 1376256 | tf_op jit(solution)/shard_map/all_to_all | solution.py:575
  39.8 0.0 copy-done.1
  39.8 14.9 %spread_direct.1 = f32[16384,128]{1,0:T(8,128)} custom-call(s32[800]{0:T(1024)} %copy-done.2, f32[2048,128]{1,0:T(8,128)} %bitcast.56), custom_call_target="tpu_custom_call" | custom-call | flops 30000001024 | bytes 100000000 | tf_op jit(solution)/shard_map/spread_direct/pallas_call | solution.py:663
  54.7 0.0 all-to-all-done.4
  54.7 0.0 copy-start.14
  54.8 0.7 convert_bitcast_fusion.head_ref
  55.4 0.2 copy-done.14
  55.7 0.0 copy-done.5
  55.7 0.0 copy-done.7
  55.7 13.7 %spread_and_turn.7 = f32[128,16,8,128]{3,2,1,0:T(8,128)} custom-call(s32[800]{0:T(1024)} %copy-done.2, s32[8,128]{1,0:T(8,128)} %convert_bitcast_fusion.head_ref, f32[1344,128]{1,0:T(8,128)} %bitcast.69, bf16[4,256,256]{2,1,0:T(8,128)(2,1)S(1)} %copy-done.5, bf16[4,256,256]{2,1,0:T(8,128)(2,1)S(1)} %copy-done.7, f32[1024,16,128]{2,1,0:T(8,128)} %bitcast.67), custom_call_target="tpu_custom_call" | custom-call | tf_op jit(solution)/shard_map/spread_and_turn/pallas_call | solution.py:616
  69.4 0.0 copy-start.3
  69.4 0.0 copy-start.8
  69.4 16.0 %all-to-all-start.5 = ((f32[128,4,2,16,128]{4,3,2,1,0:T(8,128)}), f32[128,4,2,16,128]{4,3,2,1,0:T(8,128)}, u32[]{:S(2)}, u32[]{:S(2)}) async-start(f32[128,4,2,16,128]{4,3,2,1,0:T(8,128)} %bitcast.61), calls=%async_computation.5 | async-start | bytes 16777216 | tf_op jit(solution)/shard_map/all_to_all | solution.py:575
  85.4 0.0 copy-start.6
  85.5 0.0 copy-start.13
  85.5 0.0 copy-start.15
  85.5 0.0 copy-start.16
  85.5 0.0 copy-start.17
  85.5 103.7 %all-to-all-done.5 = f32[128,4,2,16,128]{4,3,2,1,0:T(8,128)} async-done(((f32[128,4,2,16,128]{4,3,2,1,0:T(8,128)}), f32[128,4,2,16,128]{4,3,2,1,0:T(8,128)}, u32[]{:S(2)}, u32[]{:S(2)}) %all-to-all-start.5) | async-done | bytes 8388640 | tf_op jit(solution)/shard_map/all_to_all | solution.py:575
  189.2 0.0 copy-done.3
  189.2 12.3 %turn_planes.7 = (f32[2,4,512,512]{3,2,1,0:T(8,128)}, s32[1]{0:T(128)}) custom-call(f32[4,4,8,4,2,16,128]{6,5,4,3,2,1,0:T(8,128)} %bitcast.19.data_ref, bf16[4,256,256]{2,1,0:T(8,128)(2,1)S(1)} %copy-done.8, bf16[4,256,256]{2,1,0:T(8,128)(2,1)} %constant.101.clone.low_ref, bf16[1024,1024]{1,0:T(8,128)(2,1)S(1)} %copy-done.3), custom_call_target="tpu_custom_call" | custom-call | tf_op jit(solution)/shard_map/turn_planes/pallas_call | solution.py:630
  201.5 0.0 copy-done.16
  201.5 0.0 copy-done.17
  201.6 0.0 copy-done.11
  201.6 0.9 while.43
  (9 shorter events, 0.0 us)
Async XLA Ops:
  29.5 10.3 %copy-start.1 = (f32[128,16,128]{2,1,0:T(8,128)}, f32[128,16,128]{2,1,0:T(8,128)S(1)}, u32[]{:S(2)}) copy-start(f32[128,16,128]{2,1,0:T(8,128)S(1)} %all_to_all.51) | copy-start | bytes 3145732
  34.4 0.6 copy-start.2
  35.0 19.8 %all-to-all-start.4 = ((f32[8,168,128]{2,1,0:T(8,128)}), f32[8,168,128]{2,1,0:T(8,128)S(1)}, u32[]{:S(2)}, u32[]{:S(2)}) async-start(f32[8,168,128]{2,1,0:T(8,128)} %bitcast.14), calls=%async_computation.4 | async-start | bytes 1376256 | tf_op jit(solution)/shard_map/all_to_all | solution.py:575
  39.8 15.9 %copy-start.5 = (bf16[4,256,256]{2,1,0:T(8,128)(2,1)S(1)}, bf16[4,256,256]{2,1,0:T(8,128)(2,1)}, u32[]{:S(2)}) copy-start(bf16[4,256,256]{2,1,0:T(8,128)(2,1)} %constant.98.clone.high_ref) | copy-start | bytes 1572868
  39.8 15.9 %copy-start.7 = (bf16[4,256,256]{2,1,0:T(8,128)(2,1)S(1)}, bf16[4,256,256]{2,1,0:T(8,128)(2,1)}, u32[]{:S(2)}) copy-start(bf16[4,256,256]{2,1,0:T(8,128)(2,1)} %constant.99.clone.low_ref) | copy-start | bytes 1572868
  54.7 0.9 copy-start.14
  69.4 119.9 %copy-start.3 = (bf16[1024,1024]{1,0:T(8,128)(2,1)S(1)}, bf16[1024,1024]{1,0:T(8,128)(2,1)}, u32[]{:S(2)}) copy-start(bf16[1024,1024]{1,0:T(8,128)(2,1)} %constant.102.clone.y_ref) | copy-start | bytes 6291460
  69.4 119.9 %copy-start.8 = (bf16[4,256,256]{2,1,0:T(8,128)(2,1)S(1)}, bf16[4,256,256]{2,1,0:T(8,128)(2,1)}, u32[]{:S(2)}) copy-start(bf16[4,256,256]{2,1,0:T(8,128)(2,1)} %constant.100.clone.high_ref) | copy-start | bytes 1572868
  69.4 119.8 %all-to-all-start.5 = ((f32[128,4,2,16,128]{4,3,2,1,0:T(8,128)}), f32[128,4,2,16,128]{4,3,2,1,0:T(8,128)}, u32[]{:S(2)}, u32[]{:S(2)}) async-start(f32[128,4,2,16,128]{4,3,2,1,0:T(8,128)} %bitcast.61), calls=%async_computation.5 | async-start | bytes 16777216 | tf_op jit(solution)/shard_map/all_to_all | solution.py:575
  85.4 116.1 %copy-start.6 = (bf16[4,256,256]{2,1,0:T(8,128)(2,1)S(1)}, bf16[4,256,256]{2,1,0:T(8,128)(2,1)}, u32[]{:S(2)}) copy-start(bf16[4,256,256]{2,1,0:T(8,128)(2,1)} %constant.98.clone.high_ref) | copy-start | bytes 1572868
  85.5 116.1 %copy-start.13 = (f32[1,256,2,128]{3,2,1,0:T(2,128)S(1)}, f32[1,256,2,128]{3,2,1,0:T(2,128)}, u32[]{:S(2)}) copy-start(f32[1,256,2,128]{3,2,1,0:T(2,128)} %param.15) | copy-start | bytes 786436
  85.5 116.1 %copy-start.15 = (s32[1,256,1]{1,2,0:T(1,128)S(1)}, s32[1,256,1]{1,2,0:T(1,128)}, u32[]{:S(2)}) copy-start(s32[1,256,1]{1,2,0:T(1,128)} %param.16) | copy-start | bytes 3076
  85.5 116.1 %copy-start.16 = (s32[1,256]{1,0:T(1,128)S(1)}, s32[1,256]{1,0:T(1,128)}, u32[]{:S(2)}) copy-start(s32[1,256]{1,0:T(1,128)} %param.17) | copy-start | bytes 3076
  85.5 116.1 %copy-start.17 = (s32[1,256]{1,0:T(1,128)S(1)}, s32[1,256]{1,0:T(1,128)}, u32[]{:S(2)}) copy-start(s32[1,256]{1,0:T(1,128)} %param.18) | copy-start | bytes 3076
  189.2 12.3 %copy-start.11 = (f32[1,256,3,128]{3,1,2,0:T(8,128)S(1)}, f32[1,256,3,128]{3,1,2,0:T(8,128)}, u32[]{:S(2)}) copy-start(f32[1,256,3,128]{3,1,2,0:T(8,128)} %param.14) | copy-start | bytes 1179652
